TPU v7x, 32 devices: a whole 2x2x4 slice. The times are simulated.
32 devices in a mesh: member: 8 (over z, y), tile: 4 (over x, core).
Axes of the slice: x: 2, y: 2, z: 4, core: 2. Of those that a mesh axis runs over, the one named last changes fastest.
Arguments:
- features: bfloat16 [8, 128, 32, 2048], P('member', None, 'tile')
- residual_state: float32 [8, 4, 32, 2048], P('member', None, 'tile'), may hold values from -6 to 6
- noise: float32 [8, 4, 32, 2048], P('member', None, 'tile'), may hold values from -6 to 6
- regression_mean: float32 [4, 32, 2048], P(None, 'tile', 'member'), may hold values from -6 to 6
- step_index: int32 [1], replicated, may hold values from 9 to 16
- conv_first: bfloat16 [9, 128, 128], replicated, may hold values from -0.1875 to 0.1875
- conv_second: bfloat16 [9, 128, 128], replicated, may hold values from -0.1875 to 0.1875
- head_weight: bfloat16 [4, 128], replicated, may hold values from -0.5 to 0.5
- spread_target: float32 [4], replicated, may hold values from 0.5 to 4
Outputs:
- ensemble_field: float32 [8, 4, 32, 2048], P('member', None, 'tile')
- next_state: float32 [8, 4, 32, 2048], P('member', None, 'tile')
All inputs are finite; a program needn't handle non-finite values.
Results may differ from a plain program's by a relative error of at most 0.0013.
Values may be sent and summed in bfloat16 or wider, within the bound.
A program may use at most 128 MiB of HBM per device.

v0:
```python
import jax
import jax.numpy as jnp
from jax import lax
from jax.sharding import PartitionSpec as P

GROUPS = 32


def with_halo(cells, sides, width):
    for axis, dim in sides:
        count = lax.axis_size(axis)
        ends = count - 1
        head = lax.slice_in_dim(cells, 0, width, axis=dim)
        tail = lax.slice_in_dim(cells, cells.shape[dim] - width, cells.shape[dim], axis=dim)
        cells = jnp.concatenate(
            [
                lax.ppermute(tail, axis, [(i, (i + 1) % count) for i in range(ends)]),
                cells,
                lax.ppermute(head, axis, [((i + 1) % count, i) for i in range(ends)]),
            ],
            axis=dim,
        )
    return cells


def plan(step_index):
    steps = jnp.arange(18).astype(jnp.float32)
    upper = 800.0 ** (1.0 / 7.0)
    lower = 0.002 ** (1.0 / 7.0)
    sigmas = (upper + steps / 17.0 * (lower - upper)) ** 7
    places = jnp.arange(18)
    sigma = jnp.sum(jnp.where(places == step_index[0], sigmas, 0.0))
    sigma_next = jnp.sum(jnp.where(places == step_index[0] + 1, sigmas, 0.0))
    return (sigma, sigma_next)


def group_norm(block):
    height, width = (block.shape[1], block.shape[2])
    values = block.astype(jnp.float32).reshape(GROUPS, -1, height, width)
    count = values.shape[1] * height * width * lax.axis_size("tile")
    total = lax.psum(jnp.sum(values, axis=(1, 2, 3)), "tile")
    mean = total / count
    centred = values - mean[:, None, None, None]
    var = lax.psum(jnp.sum(centred * centred, axis=(1, 2, 3)), "tile") / count
    normed = centred * lax.rsqrt(var + 1e-05)[:, None, None, None]
    return jax.nn.silu(normed).astype(jnp.bfloat16).reshape(block.shape)


def convolve(activ, kernel):
    height, width = (activ.shape[1], activ.shape[2])
    bordered = with_halo(activ, (("tile", 1),), 1)
    padded = jnp.pad(bordered, ((0, 0), (0, 0), (1, 1)))
    stacked = jnp.concatenate(
        [padded[:, :, col_tap : col_tap + width] for col_tap in range(3)], axis=0
    )
    total = jnp.zeros((kernel.shape[1], height, width), jnp.float32)
    for row_tap in range(3):
        weight = jnp.concatenate([kernel[3 * row_tap + col_tap] for col_tap in range(3)], axis=1)
        window = stacked[:, row_tap : row_tap + height, :]
        total = total + jnp.einsum(
            "oc,chw->ohw", weight, window, preferred_element_type=jnp.float32
        )
    return total


def shards(
    features,
    residual_state,
    noise,
    regression_mean,
    step_index,
    conv_first,
    conv_second,
    head_weight,
    spread_target,
):
    sigma, sigma_next = plan(step_index)
    sigma_hat = 1.25 * sigma
    member_features = features[0]
    activ_first = group_norm(member_features)
    hidden_first = convolve(activ_first, conv_first).astype(jnp.bfloat16)
    activ_second = group_norm(hidden_first)
    block_out = (member_features.astype(jnp.float32) + convolve(activ_second, conv_second)).astype(
        jnp.bfloat16
    )
    network = jnp.einsum("oc,chw->ohw", head_weight, block_out, preferred_element_type=jnp.float32)
    state_hat = residual_state[0] + jnp.sqrt(sigma_hat * sigma_hat - sigma * sigma) * noise[0]
    c_skip = 0.25 / (sigma_hat * sigma_hat + 0.25)
    c_out = 0.5 * sigma_hat / jnp.sqrt(sigma_hat * sigma_hat + 0.25)
    denoised = c_skip * state_hat + c_out * network
    advanced = state_hat + (sigma_next - sigma_hat) / sigma_hat * (state_hat - denoised)
    members = features.shape[0] * lax.axis_size("member")
    target = spread_target[:, None, None]
    regional = lax.all_gather(regression_mean, "member", axis=2, tiled=True)
    first, second = lax.psum((advanced, advanced * advanced), "member")
    ens_mean = first / members
    ens_var = second / members - ens_mean * ens_mean
    factor = jnp.sqrt(1.0 + target / (ens_var + 1.0))
    field = regional + ens_mean + (advanced - ens_mean) * factor
    return (field[None], advanced[None])


def solution(mesh):
    return jax.shard_map(
        shards,
        mesh=mesh,
        in_specs=(
            P("member", None, "tile", None),
            P("member", None, "tile", None),
            P("member", None, "tile", None),
            P(None, "tile", "member"),
            P(),
            P(),
            P(),
            P(),
            P(),
        ),
        out_specs=(P("member", None, "tile", None), P("member", None, "tile", None)),
        check_vma=False,
    )
```

profile of v0, /device:TPU:16, one launch (start us, length us, event | category | flops | bytes accessed | tf_op | source)
XLA Modules:
  0.0 271.1 jit_solution(9140955397564193857)
XLA Ops:
  7.2 4.4 %convert_reduce_fusion = f32[128]{0:T(128)S(1)} fusion(bf16[1,128,8,2048]{3,2,1,0:T(8,128)(2,1)} %param.9), kind=kLoop, calls=%fused_computation.17 | loop fusion | flops 4194176 | bytes 4194816 | tf_op jit(solution)/shard_map/reduce_sum | solution.py:41
  11.9 6.9 %psum.42 = f32[32]{0:T(128)S(1)} all-reduce(f32[32]{0:T(128)S(1)} %reduce_sum.69), channel_id=1, replica_groups=mesh['member'=8,'tile'=4] {'tile'}, use_global_device_ids=true, to_apply=%region_4.5 | all-reduce | flops 32 | bytes 256 | tf_op jit(solution)/shard_map/psum | solution.py:41
  19.0 4.5 %fusion.33 = f32[128]{0:T(128)S(1)} fusion(f32[128]{0:T(128)S(1)} %sub.50, bf16[1,128,8,2048]{3,2,1,0:T(8,128)(2,1)} %param.9), kind=kLoop, calls=%fused_computation.42 | loop fusion | flops 8388480 | bytes 4195328 | tf_op jit(solution)/shard_map/reduce_sum | solution.py:44
  23.7 5.9 %psum.43 = f32[32]{0:T(128)S(1)} all-reduce(f32[32]{0:T(128)S(1)} %reduce_sum.89), channel_id=1, replica_groups=mesh['member'=8,'tile'=4] {'tile'}, use_global_device_ids=true, to_apply=%region_7.8 | all-reduce | flops 32 | bytes 256 | tf_op jit(solution)/shard_map/psum | solution.py:44
  29.7 5.4 %fusion.30 = bf16[128,8,2048]{2,0,1:T(8,128)(2,1)S(1)} fusion(f32[128]{0:T(128)S(1)} %mul.131, f32[128]{0:T(128)S(1)} %sub.50, bf16[1,128,8,2048]{3,2,1,0:T(8,128)(2,1)} %param.9), kind=kLoop, calls=%fused_computation.39 | loop fusion | flops 16777216 | bytes 8389632 | tf_op jit(solution)/shard_map/convert_element_type | solution.py:46
  40.9 7.2 %fusion.38 = bf16[128,10,2050]{2,0,1:T(8,128)(2,1)} fusion(bf16[128,1,2048]{2,0,1:T(8,128)(2,1)S(1)} %collective-permute-done.1, bf16[128,8,2048]{2,0,1:T(8,128)(2,1)S(1)} %fusion.30, bf16[128,1,2048]{2,0,1:T(8,128)(2,1)S(1)} %collective-permute-done), kind=kLoop, calls=%fused_computation.50 | loop fusion | flops 31488000 | bytes 10490880 | tf_op jit(solution)/shard_map/concatenate | solution.py:15
  48.1 10.9 %fusion.93 = (bf16[128,10,2048]{2,0,1:T(8,128)(2,1)}, bf16[128,10,2048]{2,0,1:T(8,128)(2,1)}) fusion(bf16[128,10,2050]{2,0,1:T(8,128)(2,1)} %fusion.38), kind=kLoop, calls=%fused_computation.128 | loop fusion | bytes 20971520 | tf_op jit(solution)/shard_map/slice | solution.py:54
  59.0 8.0 %pad_maximum_fusion = bf16[384,10,2048]{2,0,1:T(8,128)(2,1)S(1)} fusion(bf16[128,10,2048]{2,0,1:T(8,128)(2,1)} %get-tuple-element.13, bf16[128,1,2048]{2,0,1:T(8,128)(2,1)S(1)} %collective-permute-done.1, bf16[128,8,2048]{2,0,1:T(8,128)(2,1)} %copy-done.4, bf16[128,1,2048]{2,0,1:T(8,128)(2,1)S(1)} %collective-permute-done, ...), kind=kLoop, calls=%fused_computation.2 | loop fusion | flops 78643200 | bytes 31457280 | tf_op jit(solution)/shard_map/concatenate | solution.py:53
  67.0 5.2 %fusion.8 = f32[128,8,2048]{2,0,1:T(8,128)} fusion(bf16[384,10,2048]{2,0,1:T(8,128)(2,1)S(1)} %pad_maximum_fusion, bf16[128,128]{1,0:T(8,128)(2,1)S(1)} %get-tuple-element.28, bf16[128,128]{1,0:T(8,128)(2,1)S(1)} %get-tuple-element.29, bf16[128,128]{1,0:T(8,128)(2,1)S(1)} %get-tuple-element.30), kind=kOutput, calls=%fused_computation.12 | convolution fusion | flops 1610907648 | bytes 21069824 | tf_op jit(solution)/shard_map/oc,chw->ohw/dot_general | solution.py:60
  72.2 2.8 %copy-done.1 = bf16[384,10,2048]{2,0,1:T(8,128)(2,1)} copy-done((bf16[384,10,2048]{2,0,1:T(8,128)(2,1)}, bf16[384,10,2048]{2,0,1:T(8,128)(2,1)S(1)}, u32[]{:S(2)}) %copy-start.1) | copy-done | bytes 15728664
  75.0 4.6 %fusion.10 = f32[128,8,2048]{2,0,1:T(8,128)} fusion(bf16[384,10,2048]{2,0,1:T(8,128)(2,1)S(1)} %pad_maximum_fusion, bf16[128,128]{1,0:T(8,128)(2,1)S(1)} %get-tuple-element.31, bf16[128,128]{1,0:T(8,128)(2,1)S(1)} %get-tuple-element.32, bf16[128,128]{1,0:T(8,128)(2,1)S(1)} %get-tuple-element.33), kind=kOutput, calls=%fused_computation.14 | convolution fusion | flops 1610907648 | bytes 21069824 | tf_op jit(solution)/shard_map/oc,chw->ohw/dot_general | solution.py:60
  79.6 12.9 %convert_reduce_fusion.1 = (f32[128]{0:T(128)S(1)}, bf16[128,8,2048]{2,0,1:T(8,128)(2,1)}) fusion(bf16[384,10,2048]{2,0,1:T(8,128)(2,1)} %copy-done.1, bf16[128,128]{1,0:T(8,128)(2,1)S(1)} %get-tuple-element.34, bf16[128,128]{1,0:T(8,128)(2,1)S(1)} %get-tuple-element.35, bf16[128,128]{1,0:T(8,128)(2,1)S(1)} %get-tuple-element.27, ...), kind=kOutput, calls=%fused_computation.23 | convolution fusion | flops 1621393280 | bytes 33653248 | tf_op jit(solution)/shard_map/oc,chw->ohw/dot_general | solution.py:60
  92.8 12.8 %psum.44 = f32[32]{0:T(128)S(1)} all-reduce(f32[32]{0:T(128)S(1)} %reduce_sum.92), channel_id=1, replica_groups=mesh['member'=8,'tile'=4] {'tile'}, use_global_device_ids=true, to_apply=%region_10.11 | all-reduce | flops 32 | bytes 256 | tf_op jit(solution)/shard_map/psum | solution.py:41
  105.8 3.5 %fusion.23 = f32[128]{0:T(128)S(1)} fusion(bf16[128,8,2048]{2,0,1:T(8,128)(2,1)} %get-tuple-element.37, f32[128]{0:T(128)S(1)} %sub.56), kind=kLoop, calls=%fused_computation.32 | loop fusion | flops 8388480 | bytes 4195328 | tf_op jit(solution)/shard_map/reduce_sum | solution.py:44
  109.5 5.7 %psum.45 = f32[32]{0:T(128)S(1)} all-reduce(f32[32]{0:T(128)S(1)} %reduce_sum.95), channel_id=1, replica_groups=mesh['member'=8,'tile'=4] {'tile'}, use_global_device_ids=true, to_apply=%region_13.14 | all-reduce | flops 32 | bytes 256 | tf_op jit(solution)/shard_map/psum | solution.py:44
  115.4 4.3 %fusion.22 = bf16[128,8,2048]{2,0,1:T(8,128)(2,1)S(1)} fusion(bf16[128,8,2048]{2,0,1:T(8,128)(2,1)} %get-tuple-element.37, f32[128]{0:T(128)S(1)} %mul.137, f32[128]{0:T(128)S(1)} %sub.56), kind=kLoop, calls=%fused_computation.31 | loop fusion | flops 16777216 | bytes 8389632 | tf_op jit(solution)/shard_map/convert_element_type | solution.py:46
  130.4 6.7 %select_maximum_fusion = bf16[128,10,2050]{2,0,1:T(8,128)(2,1)} fusion(bf16[128,1,2048]{2,0,1:T(8,128)(2,1)S(1)} %collective-permute-done.3, bf16[128,8,2048]{2,0,1:T(8,128)(2,1)} %copy-done.3, bf16[128,1,2048]{2,0,1:T(8,128)(2,1)S(1)} %collective-permute-done.2), kind=kLoop, calls=%fused_computation.44 | loop fusion | flops 31488000 | bytes 10490880 | tf_op jit(solution)/shard_map/concatenate | solution.py:15
  137.2 10.9 %fusion.92 = (bf16[128,10,2048]{2,0,1:T(8,128)(2,1)}, bf16[128,10,2048]{2,0,1:T(8,128)(2,1)}) fusion(bf16[128,10,2050]{2,0,1:T(8,128)(2,1)} %select_maximum_fusion), kind=kLoop, calls=%fused_computation.127 | loop fusion | bytes 20971520 | tf_op jit(solution)/shard_map/slice | solution.py:54
  148.0 8.0 %pad_maximum_fusion.1 = bf16[384,10,2048]{2,0,1:T(8,128)(2,1)S(1)} fusion(bf16[128,10,2048]{2,0,1:T(8,128)(2,1)} %get-tuple-element.11, bf16[128,1,2048]{2,0,1:T(8,128)(2,1)S(1)} %collective-permute-done.3, bf16[128,8,2048]{2,0,1:T(8,128)(2,1)} %copy-done.3, bf16[128,1,2048]{2,0,1:T(8,128)(2,1)S(1)} %collective-permute-done.2, ...), kind=kLoop, calls=%fused_computation.3 | loop fusion | flops 78643200 | bytes 31457280 | tf_op jit(solution)/shard_map/concatenate | solution.py:53
  156.1 5.2 %fusion.2 = f32[128,8,2048]{2,0,1:T(8,128)} fusion(bf16[384,10,2048]{2,0,1:T(8,128)(2,1)S(1)} %pad_maximum_fusion.1, bf16[128,128]{1,0:T(8,128)(2,1)S(1)} %get-tuple-element.20, bf16[128,128]{1,0:T(8,128)(2,1)S(1)} %get-tuple-element.21, bf16[128,128]{1,0:T(8,128)(2,1)S(1)} %get-tuple-element.22), kind=kOutput, calls=%fused_computation.6 | convolution fusion | flops 1610907648 | bytes 21069824 | tf_op jit(solution)/shard_map/oc,chw->ohw/dot_general | solution.py:60
  164.1 4.6 %fusion = f32[128,8,2048]{2,0,1:T(8,128)} fusion(bf16[384,10,2048]{2,0,1:T(8,128)(2,1)S(1)} %pad_maximum_fusion.1, bf16[128,128]{1,0:T(8,128)(2,1)S(1)} %get-tuple-element.25, bf16[128,128]{1,0:T(8,128)(2,1)S(1)} %get-tuple-element.26, bf16[128,128]{1,0:T(8,128)(2,1)S(1)} %get-tuple-element.19), kind=kOutput, calls=%fused_computation.4 | convolution fusion | flops 1610907648 | bytes 21069824 | tf_op jit(solution)/shard_map/oc,chw->ohw/dot_general | solution.py:60
  168.7 14.8 %fusion.39 = f32[8,2048,4]{1,2,0:T(4,128)S(1)} fusion(f32[128,8,2048]{2,0,1:T(8,128)} %fusion, f32[128,8,2048]{2,0,1:T(8,128)} %fusion.2, bf16[1,128,8,2048]{3,2,1,0:T(8,128)(2,1)} %param.9, bf16[384,10,2048]{2,0,1:T(8,128)(2,1)} %copy-done.2, bf16[128,128]{1,0:T(8,128)(2,1)S(1)} %get-tuple-element.23, bf16[128,128]{1,0:T(8,128)(2,1)S(1)} %get-tuple-element.24, ...), kind=kOutput, calls=%fused_computation.51 | convolution fusion | flops 1638170624 | bytes 33915904 | tf_op jit(solution)/shard_map/oc,chw->ohw/dot_general | solution.py:86
  184.6 26.7 %all_gather.3 = f32[4,8,2048]{2,1,0:T(8,128)S(1)} all-gather(f32[4,8,256]{2,1,0:T(8,128)S(1)} %copy-done.9), channel_id=1, replica_groups=mesh['member'=8,'tile'=4] {'member'}, dimensions={2}, use_global_device_ids=true | all-gather | bytes 294912 | tf_op jit(solution)/shard_map/all_gather | solution.py:94
  211.3 50.9 %all-reduce.5.cloned.1.call-done = (f32[4,8,2048]{2,1,0:T(8,128)}, f32[4,8,2048]{2,1,0:T(8,128)}) async-done(((f32[4,8,2048]{2,1,0:T(8,128)}, f32[4,8,2048]{2,1,0:T(8,128)}), (f32[4,8,2048]{2,1,0:T(8,128)}, f32[4,8,2048]{2,1,0:T(8,128)})) %all-reduce.5.cloned.1.call-update) | async-done | bytes 524304 | tf_op jit(solution)/shard_map/psum | solution.py:95
  (59 shorter events, 19.8 us)
Async XLA Ops:
  7.2 161.5 %copy-start = (bf16[4,128]{1,0:T(4,128)(2,1)S(1)}, bf16[4,128]{1,0:T(4,128)(2,1)}, u32[]{:S(2)}) copy-start(bf16[4,128]{1,0:T(4,128)(2,1)} %param.16) | copy-start | bytes 3076
  7.2 255.0 %all-reduce.5.cloned.1.call-start = ((), (), s32[]{:S(2)}) async-start(), calls=%async_computation | async-start | bytes 1048576 | tf_op jit(solution)/shard_map/psum | solution.py:95
  11.7 26.7 %copy-start.5 = (bf16[9,128,128]{2,1,0:T(8,128)(2,1)S(1)}, bf16[9,128,128]{2,1,0:T(8,128)(2,1)}, u32[]{:S(2)}) copy-start(bf16[9,128,128]{2,1,0:T(8,128)(2,1)} %param.14) | copy-start | bytes 884740
  35.2 5.7 %copy-start.4 = (bf16[128,8,2048]{2,0,1:T(8,128)(2,1)}, bf16[128,8,2048]{2,0,1:T(8,128)(2,1)S(1)}, u32[]{:S(2)}) copy-start(bf16[128,8,2048]{2,0,1:T(8,128)(2,1)S(1)} %fusion.30) | copy-start | bytes 12582916
  35.2 3.1 %collective-permute-start = (bf16[128,1,2048]{2,0,1:T(8,128)(2,1)S(1)}, bf16[128,1,2048]{2,0,1:T(8,128)(2,1)S(1)}, u32[]{:S(2)}, u32[]{:S(2)}) collective-permute-start(bf16[128,1,2048]{2,0,1:T(8,128)(2,1)S(1)} %get-tuple-element.16), channel_id=1, source_target_pairs={{0,1},{1,2},{2,3},{4,5},{5,6},{6,7},{8,9},{9,10},{10,11},{12,13},{... | collective-permute-start | bytes 1572872 | tf_op jit(solution)/shard_map/ppermute | solution.py:17
  36.8 4.0 %collective-permute-start.1 = (bf16[128,1,2048]{2,0,1:T(8,128)(2,1)S(1)}, bf16[128,1,2048]{2,0,1:T(8,128)(2,1)S(1)}, u32[]{:S(2)}, u32[]{:S(2)}) collective-permute-start(bf16[128,1,2048]{2,0,1:T(8,128)(2,1)S(1)} %get-tuple-element.17), channel_id=1, source_target_pairs={{1,0},{2,1},{3,2},{5,4},{6,5},{7,6},{9,8},{10,9},{11,10},{13,12},{... | collective-permute-start | bytes 1572872 | tf_op jit(solution)/shard_map/ppermute | solution.py:19
  67.0 8.0 %copy-start.1 = (bf16[384,10,2048]{2,0,1:T(8,128)(2,1)}, bf16[384,10,2048]{2,0,1:T(8,128)(2,1)S(1)}, u32[]{:S(2)}) copy-start(bf16[384,10,2048]{2,0,1:T(8,128)(2,1)S(1)} %pad_maximum_fusion) | copy-start | bytes 47185924
  92.6 37.8 %copy-start.6 = (bf16[9,128,128]{2,1,0:T(8,128)(2,1)S(1)}, bf16[9,128,128]{2,1,0:T(8,128)(2,1)}, u32[]{:S(2)}) copy-start(bf16[9,128,128]{2,1,0:T(8,128)(2,1)} %param.15) | copy-start | bytes 884740
  119.7 2.0 copy-start.3
  121.8 8.7 %collective-permute-start.2 = (bf16[128,1,2048]{2,0,1:T(8,128)(2,1)S(1)}, bf16[128,1,2048]{2,0,1:T(8,128)(2,1)S(1)}, u32[]{:S(2)}, u32[]{:S(2)}) collective-permute-start(bf16[128,1,2048]{2,0,1:T(8,128)(2,1)S(1)} %get-tuple-element.14), channel_id=1, source_target_pairs={{0,1},{1,2},{2,3},{4,5},{5,6},{6,7},{8,9},{9,10},{10,11},{12,13},{... | collective-permute-start | bytes 1572872 | tf_op jit(solution)/shard_map/ppermute | solution.py:17
  123.6 6.9 %collective-permute-start.3 = (bf16[128,1,2048]{2,0,1:T(8,128)(2,1)S(1)}, bf16[128,1,2048]{2,0,1:T(8,128)(2,1)S(1)}, u32[]{:S(2)}, u32[]{:S(2)}) collective-permute-start(bf16[128,1,2048]{2,0,1:T(8,128)(2,1)S(1)} %get-tuple-element.15), channel_id=1, source_target_pairs={{1,0},{2,1},{3,2},{5,4},{6,5},{7,6},{9,8},{10,9},{11,10},{13,12},{... | collective-permute-start | bytes 1572872 | tf_op jit(solution)/shard_map/ppermute | solution.py:19
  156.1 8.0 %copy-start.2 = (bf16[384,10,2048]{2,0,1:T(8,128)(2,1)}, bf16[384,10,2048]{2,0,1:T(8,128)(2,1)S(1)}, u32[]{:S(2)}) copy-start(bf16[384,10,2048]{2,0,1:T(8,128)(2,1)S(1)} %pad_maximum_fusion.1) | copy-start | bytes 47185924
  168.7 14.8 %copy-start.7 = (f32[1,4,8,2048]{3,2,1,0:T(8,128)S(1)}, f32[1,4,8,2048]{3,2,1,0:T(8,128)}, u32[]{:S(2)}) copy-start(f32[1,4,8,2048]{3,2,1,0:T(8,128)} %param.10) | copy-start | bytes 786436
  168.7 14.8 %copy-start.8 = (f32[1,4,8,2048]{3,2,1,0:T(8,128)S(1)}, f32[1,4,8,2048]{3,2,1,0:T(8,128)}, u32[]{:S(2)}) copy-start(f32[1,4,8,2048]{3,2,1,0:T(8,128)} %param.11) | copy-start | bytes 786436
  168.7 15.8 %copy-start.9 = (f32[4,8,256]{2,1,0:T(8,128)S(1)}, f32[4,8,256]{2,1,0:T(8,128)}, u32[]{:S(2)}) copy-start(f32[4,8,256]{2,1,0:T(8,128)} %param.12) | copy-start | bytes 98308
  168.7 93.5 %copy-start.10 = (f32[4]{0:T(128)S(1)}, f32[4]{0:T(128)}, u32[]{:S(2)}) copy-start(f32[4]{0:T(128)} %param.17) | copy-start | bytes 52
Sparse Core Ops, SparseCore 0:
  184.7 77.4 all-reduce.4
where the time goes:
time: 274 us; the launch traced here: 271 us
  blocking collectives  58 us (21%)
  other arithmetic  56.8 us (21%)
  waiting for transfers between devices  53.4 us (19%)
  matrix products  47.3 us (17%)
  local copies, waits for them, and re-layouts  30.7 us (11%)
  between operations  18.4 us (7%)
  starting transfers between devices  6.41 us (2%)
    psum x1, waiting for transfers between devices, shards(): first, second = lax.psum((advanced, advanced * advanced), 'member')  50.9 us
    dot_general x5, matrix products, convolve(): jnp.einsum('oc,chw->ohw', weight, window, preferred_element_type=jnp.floa...  32.5 us
    all_gather x1, blocking collectives, shards(): regional = lax.all_gather(regression_mean, 'member', axis=2, tiled=True)  26.7 us
    slice x2, local copies, waits for them, and re-layouts, convolve(): padded[:, :, col_tap:col_tap + width]  21.7 us
    psum x2, blocking collectives, group_norm(): total = lax.psum(jnp.sum(values, axis=(1, 2, 3)), 'tile')  19.7 us
    concatenate x2, other arithmetic, convolve(): jnp.concatenate([padded[:, :, col_tap:col_tap + width] for col_tap in ran...  16.1 us
    dot_general x1, matrix products, shards(): jnp.einsum('oc,chw->ohw', head_weight, block_out, preferred_element_type=...  14.8 us
    concatenate x2, other arithmetic, with_halo(): jnp.concatenate([lax.ppermute(tail, axis, [(i, (i + 1) % count) for i in...  14 us
  transfers between devices with their start and end apart: 5, of which 2 were waited for; matrix products, arithmetic and copies ran while one was open for 0% of the time, Pallas kernels for 0%

commit v1 on v0

v1 whole, which is shorter than its diff:
```python
import functools

import jax
import jax.numpy as jnp
from jax import lax
from jax.experimental import pallas as pl
from jax.experimental.pallas import tpu as pltpu
from jax.sharding import PartitionSpec as P

GROUPS = 32
EPS = 1e-05
F32 = jnp.float32
BF16 = jnp.bfloat16
MESH = pl.DeviceIdType.MESH


def lane_to_row(column):
    n = column.shape[0]
    same = lax.broadcasted_iota(jnp.int32, (n, n), 0) == lax.broadcasted_iota(jnp.int32, (n, n), 1)
    return jnp.sum(jnp.where(same, column, 0.0), axis=0, keepdims=True)


def kernel(tiles, members, fused, chans, rows, cols, step, *refs):
    if fused:
        (coef, target, feat, resid, noise, regr, wa, wb, head, out_next, out_field) = refs[:11]
        refs = refs[11:]
    else:
        (coef, target, feat, resid, noise, wa, wb, head, out_next) = refs[:9]
        refs = refs[9:]
    (fbuf, xt, hid, act, wide, hw, perm, pivot, acc1, acc2, meanb, rstdb, stat,
     fsem, ssem, rsem, hs, hr) = refs[:18]
    if fused:
        ens_in, back_out, back_in, es, er, bs, br = refs[18:]
    me_t = lax.axis_index("tile")
    me_m = lax.axis_index("member")
    top = me_t > 0
    bottom = me_t < tiles - 1
    chunks = cols // step
    per = 256 // rows
    parts = chans // per
    pairs = rows // 2

    for k in range(parts):
        pltpu.make_async_copy(
            feat.at[pl.ds(k * 256, 256)], fbuf.at[pl.ds(k * 256, 256)], fsem.at[k]
        ).start()

    barrier = pltpu.get_barrier_semaphore()
    for d in range(1, tiles):
        pl.semaphore_signal(barrier, inc=1, device_id={"tile": lax.rem(me_t + d, tiles)}, device_id_type=MESH)
    greet = tiles - 1
    if fused:
        for d in range(1, members):
            pl.semaphore_signal(
                barrier, inc=1, device_id={"member": lax.rem(me_m + d, members)}, device_id_type=MESH
            )
        greet += members - 1

    wide[...] = jnp.zeros_like(wide)
    for which, source in enumerate((wa, wb)):
        for out_row in range(2):
            for tap_row in range(3):
                for tap_col in range(3):
                    at = (out_row + tap_row) * 3 * chans + tap_col * chans
                    wide[which, out_row * chans : (out_row + 1) * chans, at : at + chans] = source[
                        3 * tap_row + tap_col
                    ]
    hw[...] = jnp.zeros_like(hw)
    outs = head.shape[0]
    head32 = head[...].astype(F32)
    for p in range(pairs):
        for out_row in range(2):
            place = lax.broadcasted_iota(jnp.int32, (rows, chans), 0) == 2 * p + out_row
            for o in range(outs):
                hw[p, o * rows : (o + 1) * rows, out_row * chans : (out_row + 1) * chans] = jnp.where(
                    place, head32[o : o + 1, :], 0.0
                ).astype(BF16)
    to = lax.broadcasted_iota(jnp.int32, (256, 256), 0)
    frm = lax.broadcasted_iota(jnp.int32, (256, 256), 1)
    perm[...] = jnp.where((to // per == frm % rows) & (to % per == frm // rows), 1.0, 0.0).astype(BF16)
    acc1[...] = jnp.zeros_like(acc1)
    acc2[...] = jnp.zeros_like(acc2)

    def fold(values):
        total = values[:, :128]
        for at in range(128, values.shape[1], 128):
            total = total + values[:, at : at + 128]
        return total

    def accumulate(start, blocks, first):
        size = blocks[0].shape[0]
        where = pl.ds(start, size)

        @pl.when(first)
        def _():
            pivot[where, :] = jnp.broadcast_to(
                jnp.mean(blocks[0][:, :128], axis=1, keepdims=True), (size, 128)
            )

        base = pivot[where, :]
        one = jnp.zeros((size, 128), F32)
        two = jnp.zeros((size, 128), F32)
        for block in blocks:
            for at in range(0, block.shape[1], 128):
                off = block[:, at : at + 128] - base
                one = one + off
                two = two + off * off
        acc1[where, :] += one
        acc2[where, :] += two

    for k in range(parts):
        pltpu.make_async_copy(
            feat.at[pl.ds(k * 256, 256)], fbuf.at[pl.ds(k * 256, 256)], fsem.at[k]
        ).wait()

        def spread(j, carry, k=k):
            at = pl.ds(pl.multiple_of(j * step, step), step)
            moved = jnp.dot(perm[...], fbuf[k * 256 : (k + 1) * 256, at], preferred_element_type=F32)
            blocks = [moved[r * per : (r + 1) * per] for r in range(rows)]
            for r in range(rows):
                start = (1 + r) * chans + k * per
                xt[start : start + per, at] = blocks[r].astype(BF16)
            accumulate(k * per, blocks, j == 0)
            return carry

        lax.fori_loop(0, chunks, spread, 0)

    pl.semaphore_wait(barrier, greet)

    def halo(buf, turn, side):
        mine, theirs = ((1, rows + 1), (rows, 0))[side]
        return pltpu.make_async_remote_copy(
            src_ref=buf.at[pl.ds(mine * chans, chans)],
            dst_ref=buf.at[pl.ds(theirs * chans, chans)],
            send_sem=hs.at[turn, side],
            recv_sem=hr.at[turn, side],
            device_id={"tile": me_t - 1 if side == 0 else me_t + 1},
            device_id_type=MESH,
        )

    def send_halo(buf, turn, side):
        @pl.when(top if side == 0 else bottom)
        def _():
            halo(buf, turn, side).start()

    def stat_copy(turn, src, dev, d):
        return pltpu.make_async_remote_copy(
            src_ref=stat.at[turn, src],
            dst_ref=stat.at[turn, src],
            send_sem=ssem.at[turn, d],
            recv_sem=rsem.at[turn, src],
            device_id={"tile": dev},
            device_id_type=MESH,
        )

    count = rows * cols

    def norm_values(turn):
        one = jnp.sum(acc1[...], axis=1, keepdims=True)
        two = jnp.sum(acc2[...], axis=1, keepdims=True)
        mean = pivot[:, 0:1] + one / count
        dev2 = jnp.maximum(two - one * one / count, 0.0)
        row_id = lax.broadcasted_iota(jnp.int32, (8, chans), 0)
        stat[turn, me_t] = jnp.where(row_id == 0, lane_to_row(mean), lane_to_row(dev2))
        for d in range(1, tiles):
            stat_copy(turn, me_t, lax.rem(me_t + d, tiles), d).start()
        for d in range(1, tiles):
            other = lax.rem(me_t + d, tiles)
            stat_copy(turn, other, other, d).wait_recv()
        size = chans // GROUPS
        group = (
            lax.broadcasted_iota(jnp.int32, (chans, chans), 0) // size
            == lax.broadcasted_iota(jnp.int32, (chans, chans), 1) // size
        )
        every = [stat[turn, t] for t in range(tiles)]
        total = sum(one_of[0:1, :] for one_of in every)
        gmean = jnp.sum(jnp.where(group, total, 0.0), axis=1, keepdims=True) / (size * tiles)
        dev = jnp.zeros((chans, chans), F32)
        for one_of in every:
            gap = one_of[0:1, :] - gmean
            dev = dev + (one_of[1:2, :] + count * (gap * gap))
        gvar = jnp.sum(jnp.where(group, dev, 0.0), axis=1, keepdims=True) / (size * tiles * count)
        meanb[...] = jnp.broadcast_to(gmean, meanb.shape)
        rstdb[...] = jnp.broadcast_to(0.5 * lax.rsqrt(gvar + EPS), rstdb.shape)
        for d in range(1, tiles):
            stat_copy(turn, me_t, lax.rem(me_t + d, tiles), d).wait_send()

    lane = lax.broadcasted_iota(jnp.int32, (16, cols), 1)

    def activate(src, first_row, n_rows):
        def body(i, carry):
            row = first_row + i // (chans // 16)
            block = (i % (chans // 16)) * 16
            here = pl.ds(pl.multiple_of(block, 16), 16)
            value = src[pl.ds(pl.multiple_of(row * chans + block, 16), 16), :].astype(F32)
            half = (value - meanb[here, 0:1]) * rstdb[here, 0:1]
            result = half + half * jnp.tanh(half)
            before = jnp.where(lane == 0, 0.0, pltpu.roll(result, 1, 1))
            after = jnp.where(lane == cols - 1, 0.0, pltpu.roll(result, cols - 1, 1))
            for tap, one_of in enumerate((before, result, after)):
                start = pl.multiple_of(row * 3 * chans + tap * chans + block, 16)
                act[pl.ds(start, 16), :] = one_of.astype(BF16)
            return carry

        lax.fori_loop(0, n_rows * (chans // 16), body, 0)

    def activate_all(buf, turn):
        activate(buf, 1, rows)
        for side, row in ((0, rows + 1), (1, 0)):
            there = bottom if side == 0 else top

            @pl.when(there)
            def _(side=side, row=row):
                halo(buf, turn, side).wait_recv()
                activate(buf, row, 1)

            @pl.when(jnp.logical_not(there))
            def _(row=row):
                act[row * 3 * chans : (row + 1) * 3 * chans, :] = jnp.zeros((3 * chans, cols), BF16)

    def finish_halo(buf, turn):
        for side, there in ((0, top), (1, bottom)):
            @pl.when(there)
            def _(side=side):
                halo(buf, turn, side).wait_send()

    def conv(which, p, at):
        start = p * 6 * chans
        if not isinstance(p, int):
            start = pl.multiple_of(start, 128)
        return jnp.dot(wide[which], act[pl.ds(start, 12 * chans), at], preferred_element_type=F32)

    send_halo(xt, 0, 0)
    send_halo(xt, 0, 1)
    norm_values(0)
    activate_all(xt, 0)
    acc1[...] = jnp.zeros_like(acc1)
    acc2[...] = jnp.zeros_like(acc2)

    def first_conv(i, carry):
        p = lax.rem(3 * i, pairs)

        def over_cols(j, inner):
            at = pl.ds(pl.multiple_of(j * step, step), step)
            result = conv(0, p, at).astype(BF16)
            hid[pl.ds(pl.multiple_of((1 + 2 * p) * chans, chans), 2 * chans), at] = result
            wide_result = result.astype(F32)
            accumulate(0, [wide_result[:chans], wide_result[chans:]], (i == 0) & (j == 0))
            return inner

        lax.fori_loop(0, chunks, over_cols, 0)

        @pl.when(i == 0)
        def _():
            send_halo(hid, 1, 0)

        @pl.when(i == 1)
        def _():
            send_halo(hid, 1, 1)

        return carry

    lax.fori_loop(0, pairs, first_conv, 0)
    norm_values(1)
    activate_all(hid, 1)

    at_step = jnp.full((8, 128), coef[0], jnp.int32).astype(F32)
    upper = 800.0 ** (1.0 / 7.0)
    lower = 0.002 ** (1.0 / 7.0)

    def level(place):
        base = upper + place / 17.0 * (lower - upper)
        square = base * base
        return base * square * (square * square)

    sigma = level(at_step)
    sigma_next = level(at_step + 1.0)
    sigma_hat = 1.25 * sigma
    spread_of = jnp.sqrt(sigma_hat * sigma_hat - sigma * sigma)[0:1, 0:1]
    c_skip = (0.25 / (sigma_hat * sigma_hat + 0.25))[0:1, 0:1]
    c_out = (0.5 * sigma_hat / jnp.sqrt(sigma_hat * sigma_hat + 0.25))[0:1, 0:1]
    drift = ((sigma_next - sigma_hat) / sigma_hat)[0:1, 0:1]

    def advance(j):
        at = pl.ds(pl.multiple_of(j * step, step), step)
        network = jnp.zeros((outs * rows, step), F32)
        for p in range(pairs):
            start = (1 + 2 * p) * chans
            block = (xt[start : start + 2 * chans, at].astype(F32) + conv(1, p, at)).astype(BF16)
            network = network + jnp.dot(hw[p], block, preferred_element_type=F32)
        state_hat = resid[:, at] + spread_of * noise[:, at]
        denoised = c_skip * state_hat + c_out * network
        out_next[:, at] = state_hat + drift * (state_hat - denoised)

    if not fused:
        lax.fori_loop(0, chunks, lambda j, c: (advance(j), c)[1], 0)
        finish_halo(xt, 0)
        finish_halo(hid, 1)
        return

    width = cols // members
    ratio = width // step

    def state_copy(owner, sender):
        return pltpu.make_async_remote_copy(
            src_ref=out_next.at[:, pl.ds(pl.multiple_of(owner * width, width), width)],
            dst_ref=ens_in.at[sender],
            send_sem=es.at[owner],
            recv_sem=er.at[sender],
            device_id={"member": owner},
            device_id_type=MESH,
        )

    def back_copy(owner, member):
        return pltpu.make_async_remote_copy(
            src_ref=back_out,
            dst_ref=back_in.at[owner],
            send_sem=bs.at[member],
            recv_sem=br.at[owner],
            device_id={"member": member},
            device_id_type=MESH,
        )

    def ensemble():
        for d in range(1, members):
            other = lax.rem(me_m + d, members)
            state_copy(me_m, other).wait_recv()
        for o in range(outs):
            sub = pl.ds(o * rows, rows)
            one = jnp.zeros((rows, width), F32)
            two = jnp.zeros((rows, width), F32)
            for m in range(members):
                value = ens_in[m, sub, :]
                one = one + value
                two = two + value * value
            mean = one / members
            var = two / members - mean * mean
            factor = jnp.sqrt(1.0 + target[o] / (var + 1.0))
            back_out[0, sub, :] = regr[sub, :] + (mean - mean * factor)
            back_out[1, sub, :] = factor
        for d in range(1, members):
            back_copy(me_m, lax.rem(me_m + d, members)).start()
        mine = pl.ds(pl.multiple_of(me_m * width, width), width)
        out_field[:, mine] = back_out[0] + out_next[:, mine] * back_out[1]

    def turn_of(owner, carry):
        @pl.when(owner < members)
        def _():
            for part in range(ratio):
                advance(owner * ratio + part)

            @pl.when(owner != me_m)
            def _():
                state_copy(owner, me_m).start()

            @pl.when(owner == me_m)
            def _():
                ens_in[me_m] = out_next[:, pl.ds(pl.multiple_of(owner * width, width), width)]

        @pl.when(owner == me_m + 1)
        def _():
            ensemble()

        return carry

    lax.fori_loop(0, members + 1, turn_of, 0)

    def collect(d, carry):
        owner = lax.rem(me_m + d, members)
        back_copy(owner, owner).wait_recv()
        at = pl.ds(pl.multiple_of(owner * width, width), width)
        out_field[:, at] = back_in[owner, 0] + out_next[:, at] * back_in[owner, 1]
        return carry

    lax.fori_loop(1, members, collect, 0)
    for d in range(1, members):
        other = lax.rem(me_m + d, members)
        state_copy(other, me_m).wait_send()
        back_copy(me_m, other).wait_send()
    finish_halo(xt, 0)
    finish_halo(hid, 1)


def shards(
    features,
    residual_state,
    noise,
    regression_mean,
    step_index,
    conv_first,
    conv_second,
    head_weight,
    spread_target,
):
    tiles = lax.axis_size("tile")
    members = lax.axis_size("member")
    _, chans, rows, cols = features.shape
    outs = residual_state.shape[1]
    step = 256
    fused = (cols // members) % step == 0
    flat = outs * rows
    padded = rows + 2
    vmem = pl.BlockSpec(memory_space=pltpu.VMEM)
    smem = pl.BlockSpec(memory_space=pltpu.SMEM)
    operands = [
        (smem, step_index),
        (smem, spread_target),
        (pl.BlockSpec(memory_space=pl.ANY), features.reshape(chans * rows, cols)),
        (vmem, residual_state.reshape(flat, cols)),
        (vmem, noise.reshape(flat, cols)),
        (vmem, regression_mean.reshape(flat, cols // members)),
        (vmem, conv_first),
        (vmem, conv_second),
        (vmem, head_weight),
    ]
    if not fused:
        del operands[5]
    dma = pltpu.SemaphoreType.DMA
    scratch = [
        pltpu.VMEM((chans * rows, cols), BF16),
        pltpu.VMEM((padded * chans, cols), BF16),
        pltpu.VMEM((padded * chans, cols), BF16),
        pltpu.VMEM((padded * 3 * chans, cols), BF16),
        pltpu.VMEM((2, 2 * chans, 12 * chans), BF16),
        pltpu.VMEM((rows // 2, flat, 2 * chans), BF16),
        pltpu.VMEM((256, 256), BF16),
        pltpu.VMEM((chans, 128), F32),
        pltpu.VMEM((chans, 128), F32),
        pltpu.VMEM((chans, 128), F32),
        pltpu.VMEM((chans, 128), F32),
        pltpu.VMEM((chans, 128), F32),
        pltpu.VMEM((2, tiles, 8, chans), F32),
        dma((chans * rows // 256,)),
        dma((2, tiles)),
        dma((2, tiles)),
        dma((2, 2)),
        dma((2, 2)),
    ]
    if fused:
        scratch += [
            pltpu.VMEM((members, flat, cols // members), F32),
            pltpu.VMEM((2, flat, cols // members), F32),
            pltpu.VMEM((members, 2, flat, cols // members), F32),
            dma((members,)),
            dma((members,)),
            dma((members,)),
            dma((members,)),
        ]
    result = pl.pallas_call(
        functools.partial(kernel, tiles, members, fused, chans, rows, cols, step),
        out_shape=[jax.ShapeDtypeStruct((flat, cols), F32)] * (2 if fused else 1),
        in_specs=[spec for spec, _ in operands],
        out_specs=[vmem] * (2 if fused else 1),
        scratch_shapes=scratch,
        compiler_params=pltpu.CompilerParams(
            collective_id=0, has_side_effects=True, vmem_limit_bytes=52 * 1024 * 1024
        ),
    )(*[value for _, value in operands])
    advanced = result[0].reshape(outs, rows, cols)
    if fused:
        return (result[1].reshape(1, outs, rows, cols), advanced[None])
    target = spread_target[:, None, None]
    regional = lax.all_gather(regression_mean, "member", axis=2, tiled=True)
    first, second = lax.psum((advanced, advanced * advanced), "member")
    ens_mean = first / members
    ens_var = second / members - ens_mean * ens_mean
    factor = jnp.sqrt(1.0 + target / (ens_var + 1.0))
    field = regional + ens_mean + (advanced - ens_mean) * factor
    return (field[None], advanced[None])


def solution(mesh):
    return jax.shard_map(
        shards,
        mesh=mesh,
        in_specs=(
            P("member", None, "tile", None),
            P("member", None, "tile", None),
            P("member", None, "tile", None),
            P(None, "tile", "member"),
            P(),
            P(),
            P(),
            P(),
            P(),
        ),
        out_specs=(P("member", None, "tile", None), P("member", None, "tile", None)),
        check_vma=False,
    )
```

time: 274 us -> 120 us (0.44)
  Pallas kernels: 0 us -> 111 us
  blocking collectives: 58 us -> 0 us
  other arithmetic: 56.8 us -> 0 us
  waiting for transfers between devices: 53.4 us -> 0 us
  matrix products: 47.3 us -> 0 us
  local copies, waits for them, and re-layouts: 30.7 us -> 7.31 us
  between operations: 18.4 us -> 1.3 us
  starting transfers between devices: 6.41 us -> 0 us
    pallas_call x0 -> x1, Pallas kernels: none -> 111 us  [shards(): pl.pallas_call(functools.partial(kernel, tiles, members, fused, chans, ro...]
    psum x1 -> x0, waiting for transfers between devices: 50.9 us -> none  [shards(): first, second = lax.psum((advanced, advanced * advanced), 'member')]
    dot_general x6 -> x0, matrix products: 47.3 us -> none  [the longest x5 32.5 us: convolve(): jnp.einsum('oc,chw->ohw', weight, window, preferred_element_type=jnp.floa...]
    psum x4 -> x0, blocking collectives: 31.3 us -> none  [the longest x2 19.7 us: group_norm(): total = lax.psum(jnp.sum(values, axis=(1, 2, 3)), 'tile')]
    concatenate x4 -> x0, other arithmetic: 30 us -> none  [the longest x2 16.1 us: convolve(): jnp.concatenate([padded[:, :, col_tap:col_tap + width] for col_tap in ran...]
    all_gather x1 -> x0, blocking collectives: 26.7 us -> none  [shards(): regional = lax.all_gather(regression_mean, 'member', axis=2, tiled=True)]
    slice x4 -> x0, local copies, waits for them, and re-layouts: 21.9 us -> none  [the longest x2 21.7 us: convolve(): padded[:, :, col_tap:col_tap + width]]
    reduce_sum x9 -> x0, other arithmetic: 14 us -> none  [the longest x4 8.16 us: group_norm(): var = lax.psum(jnp.sum(centred * centred, axis=(1, 2, 3)), 'tile') / count]
  transfers between devices with their start and end apart: 5 -> 0, of which waited for: 2 -> 0; matrix products, arithmetic and copies ran while one was open for 0% -> 0% of each run, Pallas kernels for 0% -> 0%
where the time goes in v1:
time: 120 us; the launch traced here: 119 us
  Pallas kernels  111 us (92%)
  local copies, waits for them, and re-layouts  7.31 us (6%)
  between operations  1.3 us (1%)
    pallas_call x1, Pallas kernels, shards(): pl.pallas_call(functools.partial(kernel, tiles, members, fused, chans, ro...  111 us
    unnamed x16, local copies, waits for them, and re-layouts  7.31 us

profile of v1, /device:TPU:16, one launch (start us, length us, event | category | flops | bytes accessed | tf_op | source)
XLA Modules:
  0.0 119.2 jit_solution(15670549292258970334)
XLA Ops:
  1.3 0.0 copy-start
  1.3 1.0 copy-done
  2.2 0.0 copy-start.1
  2.2 1.0 copy-done.1
  3.2 0.0 copy-start.2
  3.2 0.9 copy-done.2
  4.2 0.0 copy-start.3
  4.2 0.9 copy-done.3
  5.1 0.0 copy-start.4
  5.1 0.8 copy-done.4
  5.9 0.0 copy-start.5
  5.9 0.7 copy-done.5
  6.5 0.0 copy-start.6
  6.5 0.7 copy-done.6
  7.2 110.5 %shard_map.104 = (f32[32,2048]{1,0:T(8,128)S(1)}, f32[32,2048]{1,0:T(8,128)S(1)}) custom-call(s32[1]{0:T(128)S(6)} %copy.13.refs_0_, f32[4]{0:T(128)S(1)} %copy-done.6, bf16[1024,2048]{1,0:T(8,128)(2,1)} %bitcast.11, f32[32,2048]{1,0:T(8,128)S(1)} %bitcast.6, f32[32,2048]{1,0:T(8,128)S(1)} %bitcast.7, f32[32,256]{1,0:T(8,128)S(1)} %bitcast.10, ...), custom_call_target="tpu_custom_call" | custom-call | tf_op jit(solution)/shard_map/pallas_call | solution.py:449
  117.7 0.7 copy.14
  118.5 0.7 copy.15
Async XLA Ops:
  1.3 1.0 copy-start
  2.2 1.0 copy-start.1
  3.2 0.9 copy-start.2
  4.2 0.9 copy-start.3
  5.1 0.8 copy-start.4
  5.9 0.7 copy-start.5
  6.5 0.7 copy-start.6

commit v2 on v1

--- a/solution.py
+++ b/solution.py
@@ -14,6 +14,11 @@
 MESH = pl.DeviceIdType.MESH
 
 
+def log2(n):
+    assert n & (n - 1) == 0
+    return n.bit_length() - 1
+
+
 def lane_to_row(column):
     n = column.shape[0]
     same = lax.broadcasted_iota(jnp.int32, (n, n), 0) == lax.broadcasted_iota(jnp.int32, (n, n), 1)
@@ -22,15 +27,17 @@
 
 def kernel(tiles, members, fused, chans, rows, cols, step, *refs):
     if fused:
-        (coef, target, feat, resid, noise, regr, wa, wb, head, out_next, out_field) = refs[:11]
+        (coef, target, feat, resid_h, noise_h, regr_h, wa_h, wb_h, head, out_next, out_field) = refs[:11]
         refs = refs[11:]
     else:
-        (coef, target, feat, resid, noise, wa, wb, head, out_next) = refs[:9]
+        (coef, target, feat, resid_h, noise_h, wa_h, wb_h, head, out_next) = refs[:9]
         refs = refs[9:]
-    (fbuf, xt, hid, act, wide, hw, perm, pivot, acc1, acc2, meanb, rstdb, stat,
-     fsem, ssem, rsem, hs, hr) = refs[:18]
+    acts = refs[: rows // 2 + 1]
+    refs = refs[rows // 2 + 1 :]
+    (fbuf, xt, hid, wide, hw, perm, pivot, acc1, acc2, meanb, rstdb, stat, resid, noise, wa, wb,
+     fsem, ssem, rsem, hs, hr, osem) = refs[:22]
     if fused:
-        ens_in, back_out, back_in, es, er, bs, br = refs[18:]
+        ens_in, back_out, back_in, regr, es, er, bs, br = refs[22:]
     me_t = lax.axis_index("tile")
     me_m = lax.axis_index("member")
     top = me_t > 0
@@ -44,6 +51,12 @@
         pltpu.make_async_copy(
             feat.at[pl.ds(k * 256, 256)], fbuf.at[pl.ds(k * 256, 256)], fsem.at[k]
         ).start()
+    pairs_of = [(wa_h, wa), (wb_h, wb), (resid_h, resid), (noise_h, noise)]
+    if fused:
+        pairs_of.append((regr_h, regr))
+    loads = [pltpu.make_async_copy(a, b, osem.at[n]) for n, (a, b) in enumerate(pairs_of)]
+    for load in loads:
+        load.start()
 
     barrier = pltpu.get_barrier_semaphore()
     for d in range(1, tiles):
@@ -56,15 +69,6 @@
             )
         greet += members - 1
 
-    wide[...] = jnp.zeros_like(wide)
-    for which, source in enumerate((wa, wb)):
-        for out_row in range(2):
-            for tap_row in range(3):
-                for tap_col in range(3):
-                    at = (out_row + tap_row) * 3 * chans + tap_col * chans
-                    wide[which, out_row * chans : (out_row + 1) * chans, at : at + chans] = source[
-                        3 * tap_row + tap_col
-                    ]
     hw[...] = jnp.zeros_like(hw)
     outs = head.shape[0]
     head32 = head[...].astype(F32)
@@ -77,7 +81,7 @@
                 ).astype(BF16)
     to = lax.broadcasted_iota(jnp.int32, (256, 256), 0)
     frm = lax.broadcasted_iota(jnp.int32, (256, 256), 1)
-    perm[...] = jnp.where((to // per == frm % rows) & (to % per == frm // rows), 1.0, 0.0).astype(BF16)
+    perm[...] = jnp.where((to & (per - 1)) * rows + (to >> log2(per)) == frm, 1.0, 0.0).astype(BF16)
     acc1[...] = jnp.zeros_like(acc1)
     acc2[...] = jnp.zeros_like(acc2)
 
@@ -91,12 +95,13 @@
         size = blocks[0].shape[0]
         where = pl.ds(start, size)
 
-        @pl.when(first)
         def _():
             pivot[where, :] = jnp.broadcast_to(
                 jnp.mean(blocks[0][:, :128], axis=1, keepdims=True), (size, 128)
             )
 
+        if first is not None:
+            pl.when(first)(_)
         base = pivot[where, :]
         one = jnp.zeros((size, 128), F32)
         two = jnp.zeros((size, 128), F32)
@@ -153,9 +158,22 @@
             device_id_type=MESH,
         )
 
+    def fill_weights():
+        wide[...] = jnp.zeros_like(wide)
+        loads[0].wait()
+        loads[1].wait()
+        for which, source in enumerate((wa, wb)):
+            for out_row in range(2):
+                for tap_row in range(3):
+                    for tap_col in range(3):
+                        at = (out_row + tap_row) * 3 * chans + tap_col * chans
+                        wide[which, out_row * chans : (out_row + 1) * chans, at : at + chans] = source[
+                            3 * tap_row + tap_col
+                        ]
+
     count = rows * cols
 
-    def norm_values(turn):
+    def norm_values(turn, meanwhile):
         one = jnp.sum(acc1[...], axis=1, keepdims=True)
         two = jnp.sum(acc2[...], axis=1, keepdims=True)
         mean = pivot[:, 0:1] + one / count
@@ -164,13 +182,14 @@
         stat[turn, me_t] = jnp.where(row_id == 0, lane_to_row(mean), lane_to_row(dev2))
         for d in range(1, tiles):
             stat_copy(turn, me_t, lax.rem(me_t + d, tiles), d).start()
+        meanwhile()
         for d in range(1, tiles):
             other = lax.rem(me_t + d, tiles)
             stat_copy(turn, other, other, d).wait_recv()
         size = chans // GROUPS
         group = (
-            lax.broadcasted_iota(jnp.int32, (chans, chans), 0) // size
-            == lax.broadcasted_iota(jnp.int32, (chans, chans), 1) // size
+            lax.broadcasted_iota(jnp.int32, (chans, chans), 0) >> log2(size)
+            == lax.broadcasted_iota(jnp.int32, (chans, chans), 1) >> log2(size)
         )
         every = [stat[turn, t] for t in range(tiles)]
         total = sum(one_of[0:1, :] for one_of in every)
@@ -185,38 +204,45 @@
         for d in range(1, tiles):
             stat_copy(turn, me_t, lax.rem(me_t + d, tiles), d).wait_send()
 
-    lane = lax.broadcasted_iota(jnp.int32, (16, cols), 1)
-
-    def activate(src, first_row, n_rows):
-        def body(i, carry):
-            row = first_row + i // (chans // 16)
-            block = (i % (chans // 16)) * 16
-            here = pl.ds(pl.multiple_of(block, 16), 16)
-            value = src[pl.ds(pl.multiple_of(row * chans + block, 16), 16), :].astype(F32)
-            half = (value - meanb[here, 0:1]) * rstdb[here, 0:1]
-            result = half + half * jnp.tanh(half)
-            before = jnp.where(lane == 0, 0.0, pltpu.roll(result, 1, 1))
-            after = jnp.where(lane == cols - 1, 0.0, pltpu.roll(result, cols - 1, 1))
-            for tap, one_of in enumerate((before, result, after)):
-                start = pl.multiple_of(row * 3 * chans + tap * chans + block, 16)
-                act[pl.ds(start, 16), :] = one_of.astype(BF16)
+    edge_lane = lax.broadcasted_iota(jnp.int32, (16, 128), 1)
+    blocks_of = chans // 16
+
+    def activate_block(src, row, block):
+        here = pl.ds(pl.multiple_of(block * 16, 16), 16)
+        value = src[pl.ds(pl.multiple_of(row * chans + block * 16, 16), 16), :].astype(F32)
+        half = (value - meanb[here, 0:1]) * rstdb[here, 0:1]
+        result = (half + half * jnp.tanh(half)).astype(BF16)
+        before = pltpu.roll(result, 1, 1)
+        after = pltpu.roll(result, cols - 1, 1)
+        into = acts[row // 2]
+        for tap, one_of in enumerate((before, result, after)):
+            start = pl.multiple_of(((row % 2) * 3 + tap) * chans + block * 16, 16)
+            into[pl.ds(start, 16), :] = one_of
+            if tap != 1:
+                lanes = slice(0, 128) if tap == 0 else slice(cols - 128, cols)
+                keep = edge_lane != (0 if tap == 0 else 127)
+                part = one_of[:, lanes].astype(F32)
+                into[pl.ds(start, 16), lanes] = jnp.where(keep, part, 0.0).astype(BF16)
+
+    def activate(src, row):
+        def body(block, carry):
+            activate_block(src, row, block)
             return carry
 
-        lax.fori_loop(0, n_rows * (chans // 16), body, 0)
-
-    def activate_all(buf, turn):
-        activate(buf, 1, rows)
-        for side, row in ((0, rows + 1), (1, 0)):
-            there = bottom if side == 0 else top
-
-            @pl.when(there)
-            def _(side=side, row=row):
-                halo(buf, turn, side).wait_recv()
-                activate(buf, row, 1)
-
-            @pl.when(jnp.logical_not(there))
-            def _(row=row):
-                act[row * 3 * chans : (row + 1) * 3 * chans, :] = jnp.zeros((3 * chans, cols), BF16)
+        lax.fori_loop(0, blocks_of, body, 0)
+
+    def activate_edge(buf, turn, row):
+        side, there = (1, top) if row == 0 else (0, bottom)
+
+        @pl.when(there)
+        def _():
+            halo(buf, turn, side).wait_recv()
+            activate(buf, row)
+
+        @pl.when(jnp.logical_not(there))
+        def _():
+            start = (row % 2) * 3 * chans
+            acts[row // 2][start : start + 3 * chans, :] = jnp.zeros((3 * chans, cols), BF16)
 
     def finish_halo(buf, turn):
         for side, there in ((0, top), (1, bottom)):
@@ -225,44 +251,52 @@
                 halo(buf, turn, side).wait_send()
 
     def conv(which, p, at):
-        start = p * 6 * chans
-        if not isinstance(p, int):
-            start = pl.multiple_of(start, 128)
-        return jnp.dot(wide[which], act[pl.ds(start, 12 * chans), at], preferred_element_type=F32)
+        half = 6 * chans
+        return jnp.dot(wide[which, :, :half], acts[p][:, at], preferred_element_type=F32) + jnp.dot(
+            wide[which, :, half:], acts[p + 1][:, at], preferred_element_type=F32
+        )
 
     send_halo(xt, 0, 0)
     send_halo(xt, 0, 1)
-    norm_values(0)
-    activate_all(xt, 0)
+    norm_values(0, fill_weights)
     acc1[...] = jnp.zeros_like(acc1)
     acc2[...] = jnp.zeros_like(acc2)
 
-    def first_conv(i, carry):
-        p = lax.rem(3 * i, pairs)
-
-        def over_cols(j, inner):
+    def first_conv(p, first, beside):
+        total = len(beside) * blocks_of // chunks
+
+        def over_cols(j, carry):
             at = pl.ds(pl.multiple_of(j * step, step), step)
             result = conv(0, p, at).astype(BF16)
-            hid[pl.ds(pl.multiple_of((1 + 2 * p) * chans, chans), 2 * chans), at] = result
+            for row in beside:
+                for n in range(total // len(beside)):
+                    activate_block(xt, row, j * (total // len(beside)) + n)
+            start = (1 + 2 * p) * chans
+            hid[start : start + 2 * chans, at] = result
             wide_result = result.astype(F32)
-            accumulate(0, [wide_result[:chans], wide_result[chans:]], (i == 0) & (j == 0))
-            return inner
+            accumulate(0, [wide_result[:chans], wide_result[chans:]], (j == 0) if first else None)
+            return carry
 
         lax.fori_loop(0, chunks, over_cols, 0)
 
-        @pl.when(i == 0)
-        def _():
-            send_halo(hid, 1, 0)
-
-        @pl.when(i == 1)
-        def _():
-            send_halo(hid, 1, 1)
-
-        return carry
-
-    lax.fori_loop(0, pairs, first_conv, 0)
-    norm_values(1)
-    activate_all(hid, 1)
+    for row in (1, 2, 3):
+        activate(xt, row)
+    activate_edge(xt, 0, 0)
+    first_conv(0, True, [rows - 2, rows - 1, rows])
+    send_halo(hid, 1, 0)
+    activate_edge(xt, 0, rows + 1)
+    middle = list(range(4, rows - 2))
+    first_conv(pairs - 1, False, middle)
+    send_halo(hid, 1, 1)
+    for p in range(1, pairs - 1):
+        first_conv(p, False, [])
+    norm_values(1, lambda: None)
+    for row in range(1, rows + 1):
+        activate(hid, row)
+    activate_edge(hid, 1, 0)
+    activate_edge(hid, 1, rows + 1)
+    for load in loads[2:]:
+        load.wait()
 
     at_step = jnp.full((8, 128), coef[0], jnp.int32).astype(F32)
     upper = 800.0 ** (1.0 / 7.0)
@@ -402,25 +436,25 @@
     padded = rows + 2
     vmem = pl.BlockSpec(memory_space=pltpu.VMEM)
     smem = pl.BlockSpec(memory_space=pltpu.SMEM)
+    anywhere = pl.BlockSpec(memory_space=pl.ANY)
     operands = [
         (smem, step_index),
         (smem, spread_target),
-        (pl.BlockSpec(memory_space=pl.ANY), features.reshape(chans * rows, cols)),
-        (vmem, residual_state.reshape(flat, cols)),
-        (vmem, noise.reshape(flat, cols)),
-        (vmem, regression_mean.reshape(flat, cols // members)),
-        (vmem, conv_first),
-        (vmem, conv_second),
+        (anywhere, features.reshape(chans * rows, cols)),
+        (anywhere, residual_state.reshape(flat, cols)),
+        (anywhere, noise.reshape(flat, cols)),
+        (anywhere, regression_mean.reshape(flat, cols // members)),
+        (anywhere, conv_first),
+        (anywhere, conv_second),
         (vmem, head_weight),
     ]
     if not fused:
         del operands[5]
     dma = pltpu.SemaphoreType.DMA
-    scratch = [
+    scratch = [pltpu.VMEM((6 * chans, cols), BF16) for _ in range(rows // 2 + 1)] + [
         pltpu.VMEM((chans * rows, cols), BF16),
         pltpu.VMEM((padded * chans, cols), BF16),
         pltpu.VMEM((padded * chans, cols), BF16),
-        pltpu.VMEM((padded * 3 * chans, cols), BF16),
         pltpu.VMEM((2, 2 * chans, 12 * chans), BF16),
         pltpu.VMEM((rows // 2, flat, 2 * chans), BF16),
         pltpu.VMEM((256, 256), BF16),
@@ -430,17 +464,23 @@
         pltpu.VMEM((chans, 128), F32),
         pltpu.VMEM((chans, 128), F32),
         pltpu.VMEM((2, tiles, 8, chans), F32),
+        pltpu.VMEM((flat, cols), F32),
+        pltpu.VMEM((flat, cols), F32),
+        pltpu.VMEM(conv_first.shape, BF16),
+        pltpu.VMEM(conv_second.shape, BF16),
         dma((chans * rows // 256,)),
         dma((2, tiles)),
         dma((2, tiles)),
         dma((2, 2)),
         dma((2, 2)),
+        dma((5,)),
     ]
     if fused:
         scratch += [
             pltpu.VMEM((members, flat, cols // members), F32),
             pltpu.VMEM((2, flat, cols // members), F32),
             pltpu.VMEM((members, 2, flat, cols // members), F32),
+            pltpu.VMEM((flat, cols // members), F32),
             dma((members,)),
             dma((members,)),
             dma((members,)),

time: 120 us -> 111 us (0.925)
  Pallas kernels: 111 us -> 102 us
    pallas_call x1, Pallas kernels: 111 us -> 102 us  [shards(): pl.pallas_call(functools.partial(kernel, tiles, members, fused, chans, ro...]
where the time goes in v2:
time: 111 us; the launch traced here: 110 us
  Pallas kernels  102 us (92%)
  local copies, waits for them, and re-layouts  7.31 us (7%)
  between operations  1.3 us (1%)
    pallas_call x1, Pallas kernels, shards(): pl.pallas_call(functools.partial(kernel, tiles, members, fused, chans, ro...  102 us
    unnamed x16, local copies, waits for them, and re-layouts  7.31 us

profile of v2, /device:TPU:16, one launch (start us, length us, event | category | flops | bytes accessed | tf_op | source)
XLA Modules:
  0.0 110.4 jit_solution(13315760575545021271)
XLA Ops:
  1.3 0.0 copy-start
  1.3 1.0 copy-done
  2.2 0.0 copy-start.1
  2.2 1.0 copy-done.1
  3.2 0.0 copy-start.2
  3.2 0.9 copy-done.2
  4.2 0.0 copy-start.3
  4.2 0.9 copy-done.3
  5.1 0.0 copy-start.4
  5.1 0.8 copy-done.4
  5.9 0.0 copy-start.5
  5.9 0.7 copy-done.5
  6.5 0.0 copy-start.6
  6.5 0.7 copy-done.6
  7.2 101.8 %shard_map.104 = (f32[32,2048]{1,0:T(8,128)S(1)}, f32[32,2048]{1,0:T(8,128)S(1)}) custom-call(s32[1]{0:T(128)S(6)} %copy.13.refs_0_, f32[4]{0:T(128)S(1)} %copy-done.6, bf16[1024,2048]{1,0:T(8,128)(2,1)} %bitcast.11, f32[32,2048]{1,0:T(8,128)S(1)} %bitcast.6, f32[32,2048]{1,0:T(8,128)S(1)} %bitcast.7, f32[32,256]{1,0:T(8,128)S(1)} %bitcast.10, ...), custom_call_target="tpu_custom_call" | custom-call | tf_op jit(solution)/shard_map/pallas_call | solution.py:489
  109.0 0.7 copy.14
  109.7 0.7 copy.15
Async XLA Ops:
  1.3 1.0 copy-start
  2.2 1.0 copy-start.1
  3.2 0.9 copy-start.2
  4.2 0.9 copy-start.3
  5.1 0.8 copy-start.4
  5.9 0.7 copy-start.5
  6.5 0.7 copy-start.6

commit v3 on v2

--- a/solution.py
+++ b/solution.py
@@ -12,6 +12,7 @@
 F32 = jnp.float32
 BF16 = jnp.bfloat16
 MESH = pl.DeviceIdType.MESH
+LAG = 128
 
 
 def log2(n):
@@ -35,9 +36,9 @@
     acts = refs[: rows // 2 + 1]
     refs = refs[rows // 2 + 1 :]
     (fbuf, xt, hid, wide, hw, perm, pivot, acc1, acc2, meanb, rstdb, stat, resid, noise, wa, wb,
-     fsem, ssem, rsem, hs, hr, osem) = refs[:22]
+     pend, carry_m, state, fsem, ssem, rsem, hs, hr, osem) = refs[:25]
     if fused:
-        ens_in, back_out, back_in, regr, es, er, bs, br = refs[22:]
+        ens_in, back_out, back_in, regr, field, es, er, bs, br = refs[25:]
     me_t = lax.axis_index("tile")
     me_m = lax.axis_index("member")
     top = me_t > 0
@@ -51,7 +52,8 @@
         pltpu.make_async_copy(
             feat.at[pl.ds(k * 256, 256)], fbuf.at[pl.ds(k * 256, 256)], fsem.at[k]
         ).start()
-    pairs_of = [(wa_h, wa), (wb_h, wb), (resid_h, resid), (noise_h, noise)]
+    inner = pl.ds(LAG, cols)
+    pairs_of = [(wa_h, wa), (wb_h, wb), (resid_h, resid.at[:, inner]), (noise_h, noise.at[:, inner])]
     if fused:
         pairs_of.append((regr_h, regr))
     loads = [pltpu.make_async_copy(a, b, osem.at[n]) for n, (a, b) in enumerate(pairs_of)]
@@ -100,7 +102,9 @@
                 jnp.mean(blocks[0][:, :128], axis=1, keepdims=True), (size, 128)
             )
 
-        if first is not None:
+        if first is True:
+            _()
+        elif first is not None:
             pl.when(first)(_)
         base = pivot[where, :]
         one = jnp.zeros((size, 128), F32)
@@ -124,7 +128,7 @@
             blocks = [moved[r * per : (r + 1) * per] for r in range(rows)]
             for r in range(rows):
                 start = (1 + r) * chans + k * per
-                xt[start : start + per, at] = blocks[r].astype(BF16)
+                xt[start : start + per, pl.ds(pl.multiple_of(j * step + LAG, LAG), step)] = blocks[r].astype(BF16)
             accumulate(k * per, blocks, j == 0)
             return carry
 
@@ -135,8 +139,8 @@
     def halo(buf, turn, side):
         mine, theirs = ((1, rows + 1), (rows, 0))[side]
         return pltpu.make_async_remote_copy(
-            src_ref=buf.at[pl.ds(mine * chans, chans)],
-            dst_ref=buf.at[pl.ds(theirs * chans, chans)],
+            src_ref=buf.at[pl.ds(mine * chans, chans), pl.ds(LAG, cols)],
+            dst_ref=buf.at[pl.ds(theirs * chans, chans), pl.ds(LAG, cols)],
             send_sem=hs.at[turn, side],
             recv_sem=hr.at[turn, side],
             device_id={"tile": me_t - 1 if side == 0 else me_t + 1},
@@ -166,8 +170,9 @@
             for out_row in range(2):
                 for tap_row in range(3):
                     for tap_col in range(3):
-                        at = (out_row + tap_row) * 3 * chans + tap_col * chans
-                        wide[which, out_row * chans : (out_row + 1) * chans, at : at + chans] = source[
+                        at = (out_row + tap_row) * chans
+                        to_row = (2 * tap_col + out_row) * chans
+                        wide[which, to_row : to_row + chans, at : at + chans] = source[
                             3 * tap_row + tap_col
                         ]
 
@@ -204,25 +209,14 @@
         for d in range(1, tiles):
             stat_copy(turn, me_t, lax.rem(me_t + d, tiles), d).wait_send()
 
-    edge_lane = lax.broadcasted_iota(jnp.int32, (16, 128), 1)
     blocks_of = chans // 16
 
     def activate_block(src, row, block):
         here = pl.ds(pl.multiple_of(block * 16, 16), 16)
-        value = src[pl.ds(pl.multiple_of(row * chans + block * 16, 16), 16), :].astype(F32)
+        value = src[pl.ds(pl.multiple_of(row * chans + block * 16, 16), 16), LAG:].astype(F32)
         half = (value - meanb[here, 0:1]) * rstdb[here, 0:1]
-        result = (half + half * jnp.tanh(half)).astype(BF16)
-        before = pltpu.roll(result, 1, 1)
-        after = pltpu.roll(result, cols - 1, 1)
-        into = acts[row // 2]
-        for tap, one_of in enumerate((before, result, after)):
-            start = pl.multiple_of(((row % 2) * 3 + tap) * chans + block * 16, 16)
-            into[pl.ds(start, 16), :] = one_of
-            if tap != 1:
-                lanes = slice(0, 128) if tap == 0 else slice(cols - 128, cols)
-                keep = edge_lane != (0 if tap == 0 else 127)
-                part = one_of[:, lanes].astype(F32)
-                into[pl.ds(start, 16), lanes] = jnp.where(keep, part, 0.0).astype(BF16)
+        start = pl.multiple_of((row % 2) * chans + block * 16, 16)
+        acts[row // 2][pl.ds(start, 16), :] = (half + half * jnp.tanh(half)).astype(BF16)
 
     def activate(src, row):
         def body(block, carry):
@@ -241,8 +235,8 @@
 
         @pl.when(jnp.logical_not(there))
         def _():
-            start = (row % 2) * 3 * chans
-            acts[row // 2][start : start + 3 * chans, :] = jnp.zeros((3 * chans, cols), BF16)
+            start = (row % 2) * chans
+            acts[row // 2][start : start + chans, :] = jnp.zeros((chans, cols), BF16)
 
     def finish_halo(buf, turn):
         for side, there in ((0, top), (1, bottom)):
@@ -250,11 +244,30 @@
             def _(side=side):
                 halo(buf, turn, side).wait_send()
 
-    def conv(which, p, at):
-        half = 6 * chans
-        return jnp.dot(wide[which, :, :half], acts[p][:, at], preferred_element_type=F32) + jnp.dot(
-            wide[which, :, half:], acts[p + 1][:, at], preferred_element_type=F32
-        )
+    lane = lax.broadcasted_iota(jnp.int32, (2 * chans, LAG), 1)
+
+    def conv(which, p, slot, at):
+        taps = jnp.dot(
+            wide[which],
+            jnp.concatenate([acts[p][:, at], acts[p + 1][:, at]], axis=0),
+            preferred_element_type=F32,
+        )
+        left, centre, right = (taps[n * 2 * chans : (n + 1) * 2 * chans] for n in range(3))
+        left0, left1 = (pltpu.roll(left[:, n : n + LAG], 1, 1) for n in (0, LAG))
+        right0, right1 = (pltpu.roll(right[:, n : n + LAG], LAG - 1, 1) for n in (0, LAG))
+        before = pend[slot] + jnp.where(lane == LAG - 1, right0, 0.0)
+        first = (
+            centre[:, :LAG]
+            + jnp.where(lane == 0, carry_m[slot], left0)
+            + jnp.where(lane == LAG - 1, right1, right0)
+        )
+        pend[slot] = (
+            centre[:, LAG:]
+            + jnp.where(lane == 0, left0, left1)
+            + jnp.where(lane == LAG - 1, 0.0, right1)
+        )
+        carry_m[slot] = left1
+        return before, first
 
     send_halo(xt, 0, 0)
     send_halo(xt, 0, 1)
@@ -263,21 +276,37 @@
     acc2[...] = jnp.zeros_like(acc2)
 
     def first_conv(p, first, beside):
-        total = len(beside) * blocks_of // chunks
+        each = blocks_of // chunks
+        rows_at = slice((1 + 2 * p) * chans, (3 + 2 * p) * chans)
+        pend[0] = jnp.zeros_like(pend[0])
+        carry_m[0] = jnp.zeros_like(carry_m[0])
+
+        def keep(blocks, starts, pivot_now):
+            kept = []
+            for block, start in zip(blocks, starts):
+                rounded = block.astype(BF16)
+                hid[rows_at, pl.ds(start, LAG)] = rounded
+                wide_block = rounded.astype(F32)
+                kept += [wide_block[:chans], wide_block[chans:]]
+            accumulate(0, kept, pivot_now)
 
         def over_cols(j, carry):
-            at = pl.ds(pl.multiple_of(j * step, step), step)
-            result = conv(0, p, at).astype(BF16)
+            base = j * step
+            if not isinstance(j, int):
+                base = pl.multiple_of(base, step)
+            blocks = conv(0, p, 0, pl.ds(base, step))
             for row in beside:
-                for n in range(total // len(beside)):
-                    activate_block(xt, row, j * (total // len(beside)) + n)
-            start = (1 + 2 * p) * chans
-            hid[start : start + 2 * chans, at] = result
-            wide_result = result.astype(F32)
-            accumulate(0, [wide_result[:chans], wide_result[chans:]], (j == 0) if first else None)
+                for n in range(each):
+                    activate_block(xt, row, j * each + n)
+            if isinstance(j, int):
+                keep(blocks[1:], [LAG], True if first else None)
+            else:
+                keep(blocks, [base, pl.multiple_of(base + LAG, LAG)], None)
             return carry
 
-        lax.fori_loop(0, chunks, over_cols, 0)
+        over_cols(0, 0)
+        lax.fori_loop(1, chunks, over_cols, 0)
+        keep([pend[0]], [cols], None)
 
     for row in (1, 2, 3):
         activate(xt, row)
@@ -315,19 +344,35 @@
     c_out = (0.5 * sigma_hat / jnp.sqrt(sigma_hat * sigma_hat + 0.25))[0:1, 0:1]
     drift = ((sigma_next - sigma_hat) / sigma_hat)[0:1, 0:1]
 
-    def advance(j):
-        at = pl.ds(pl.multiple_of(j * step, step), step)
-        network = jnp.zeros((outs * rows, step), F32)
+    def advance(blocks_of_pair, start, size):
+        at = pl.ds(start, size)
+        network = jnp.zeros((outs * rows, size), F32)
         for p in range(pairs):
-            start = (1 + 2 * p) * chans
-            block = (xt[start : start + 2 * chans, at].astype(F32) + conv(1, p, at)).astype(BF16)
+            first_row = (1 + 2 * p) * chans
+            block = (xt[first_row : first_row + 2 * chans, at].astype(F32) + blocks_of_pair(p)).astype(BF16)
             network = network + jnp.dot(hw[p], block, preferred_element_type=F32)
         state_hat = resid[:, at] + spread_of * noise[:, at]
         denoised = c_skip * state_hat + c_out * network
-        out_next[:, at] = state_hat + drift * (state_hat - denoised)
+        state[:, at] = state_hat + drift * (state_hat - denoised)
+
+    pend[...] = jnp.zeros_like(pend)
+    carry_m[...] = jnp.zeros_like(carry_m)
+
+    def window(j):
+        base = pl.multiple_of(j * step, step)
+        advance(lambda p: jnp.concatenate(conv(1, p, p, pl.ds(base, step)), axis=1), base, step)
+
+    def last_window():
+        advance(lambda p: pend[p], cols, LAG)
+
+    def state_out():
+        return pltpu.make_async_copy(state.at[:, inner], out_next, osem.at[0])
 
     if not fused:
-        lax.fori_loop(0, chunks, lambda j, c: (advance(j), c)[1], 0)
+        lax.fori_loop(0, chunks, lambda j, c: (window(j), c)[1], 0)
+        last_window()
+        state_out().start()
+        state_out().wait()
         finish_halo(xt, 0)
         finish_halo(hid, 1)
         return
@@ -335,9 +380,15 @@
     width = cols // members
     ratio = width // step
 
+    def owned(owner):
+        start = owner * width + LAG
+        if not isinstance(start, int):
+            start = pl.multiple_of(start, LAG)
+        return pl.ds(start, width)
+
     def state_copy(owner, sender):
         return pltpu.make_async_remote_copy(
-            src_ref=out_next.at[:, pl.ds(pl.multiple_of(owner * width, width), width)],
+            src_ref=state.at[:, owned(owner)],
             dst_ref=ens_in.at[sender],
             send_sem=es.at[owner],
             recv_sem=er.at[sender],
@@ -375,44 +426,58 @@
         for d in range(1, members):
             back_copy(me_m, lax.rem(me_m + d, members)).start()
         mine = pl.ds(pl.multiple_of(me_m * width, width), width)
-        out_field[:, mine] = back_out[0] + out_next[:, mine] * back_out[1]
-
-    def turn_of(owner, carry):
-        @pl.when(owner < members)
-        def _():
-            for part in range(ratio):
-                advance(owner * ratio + part)
-
-            @pl.when(owner != me_m)
-            def _():
-                state_copy(owner, me_m).start()
-
-            @pl.when(owner == me_m)
-            def _():
-                ens_in[me_m] = out_next[:, pl.ds(pl.multiple_of(owner * width, width), width)]
-
-        @pl.when(owner == me_m + 1)
+        field[:, mine] = back_out[0] + state[:, owned(me_m)] * back_out[1]
+
+    def hand_over(owner):
+        @pl.when(owner != me_m)
+        def _():
+            state_copy(owner, me_m).start()
+
+        @pl.when(owner == me_m)
+        def _():
+            ens_in[me_m] = state[:, owned(owner)]
+
+    def turn_of(j, carry):
+        window(j)
+
+        @pl.when((j >= ratio) & (j % ratio == 0))
+        def _():
+            hand_over(j // ratio - 1)
+
+        @pl.when(j == (me_m + 1) * ratio + 1)
         def _():
             ensemble()
 
         return carry
 
-    lax.fori_loop(0, members + 1, turn_of, 0)
+    lax.fori_loop(0, chunks, turn_of, 0)
+    last_window()
+    hand_over(members - 1)
+
+    @pl.when((me_m + 1) * ratio + 1 >= chunks)
+    def _():
+        ensemble()
+
+    state_out().start()
 
     def collect(d, carry):
         owner = lax.rem(me_m + d, members)
         back_copy(owner, owner).wait_recv()
         at = pl.ds(pl.multiple_of(owner * width, width), width)
-        out_field[:, at] = back_in[owner, 0] + out_next[:, at] * back_in[owner, 1]
+        field[:, at] = back_in[owner, 0] + state[:, owned(owner)] * back_in[owner, 1]
         return carry
 
     lax.fori_loop(1, members, collect, 0)
+    field_out = pltpu.make_async_copy(field, out_field, osem.at[1])
+    field_out.start()
     for d in range(1, members):
         other = lax.rem(me_m + d, members)
         state_copy(other, me_m).wait_send()
         back_copy(me_m, other).wait_send()
     finish_halo(xt, 0)
     finish_halo(hid, 1)
+    state_out().wait()
+    field_out.wait()
 
 
 def shards(
@@ -451,11 +516,11 @@
     if not fused:
         del operands[5]
     dma = pltpu.SemaphoreType.DMA
-    scratch = [pltpu.VMEM((6 * chans, cols), BF16) for _ in range(rows // 2 + 1)] + [
+    scratch = [pltpu.VMEM((2 * chans, cols), BF16) for _ in range(rows // 2 + 1)] + [
         pltpu.VMEM((chans * rows, cols), BF16),
-        pltpu.VMEM((padded * chans, cols), BF16),
-        pltpu.VMEM((padded * chans, cols), BF16),
-        pltpu.VMEM((2, 2 * chans, 12 * chans), BF16),
+        pltpu.VMEM((padded * chans, LAG + cols), BF16),
+        pltpu.VMEM((padded * chans, LAG + cols), BF16),
+        pltpu.VMEM((2, 6 * chans, 4 * chans), BF16),
         pltpu.VMEM((rows // 2, flat, 2 * chans), BF16),
         pltpu.VMEM((256, 256), BF16),
         pltpu.VMEM((chans, 128), F32),
@@ -464,10 +529,13 @@
         pltpu.VMEM((chans, 128), F32),
         pltpu.VMEM((chans, 128), F32),
         pltpu.VMEM((2, tiles, 8, chans), F32),
-        pltpu.VMEM((flat, cols), F32),
-        pltpu.VMEM((flat, cols), F32),
+        pltpu.VMEM((flat, LAG + cols), F32),
+        pltpu.VMEM((flat, LAG + cols), F32),
         pltpu.VMEM(conv_first.shape, BF16),
         pltpu.VMEM(conv_second.shape, BF16),
+        pltpu.VMEM((rows // 2, 2 * chans, LAG), F32),
+        pltpu.VMEM((rows // 2, 2 * chans, LAG), F32),
+        pltpu.VMEM((flat, LAG + cols), F32),
         dma((chans * rows // 256,)),
         dma((2, tiles)),
         dma((2, tiles)),
@@ -481,6 +549,7 @@
             pltpu.VMEM((2, flat, cols // members), F32),
             pltpu.VMEM((members, 2, flat, cols // members), F32),
             pltpu.VMEM((flat, cols // members), F32),
+            pltpu.VMEM((flat, cols), F32),
             dma((members,)),
             dma((members,)),
             dma((members,)),
@@ -490,7 +559,7 @@
         functools.partial(kernel, tiles, members, fused, chans, rows, cols, step),
         out_shape=[jax.ShapeDtypeStruct((flat, cols), F32)] * (2 if fused else 1),
         in_specs=[spec for spec, _ in operands],
-        out_specs=[vmem] * (2 if fused else 1),
+        out_specs=[anywhere] * (2 if fused else 1),
         scratch_shapes=scratch,
         compiler_params=pltpu.CompilerParams(
             collective_id=0, has_side_effects=True, vmem_limit_bytes=52 * 1024 * 1024

time: 111 us -> 103 us (0.928)
  Pallas kernels: 102 us -> 94.2 us
    pallas_call x1, Pallas kernels: 102 us -> 94.2 us  [shards(): pl.pallas_call(functools.partial(kernel, tiles, members, fused, chans, ro...]
where the time goes in v3:
time: 103 us
  Pallas kernels  94.2 us (91%)
  local copies, waits for them, and re-layouts  7.31 us (7%)
  between operations  1.3 us (1%)
    pallas_call x1, Pallas kernels, shards(): pl.pallas_call(functools.partial(kernel, tiles, members, fused, chans, ro...  94.2 us
    unnamed x16, local copies, waits for them, and re-layouts  7.31 us

profile of v3, /device:TPU:16, one launch (start us, length us, event | category | flops | bytes accessed | tf_op | source)
XLA Modules:
  0.0 102.8 jit_solution(4971821510633927340)
XLA Ops:
  1.3 0.0 copy-start
  1.3 1.0 copy-done
  2.2 0.0 copy-start.1
  2.2 1.0 copy-done.1
  3.2 0.0 copy-start.2
  3.2 0.9 copy-done.2
  4.2 0.0 copy-start.3
  4.2 0.9 copy-done.3
  5.1 0.0 copy-start.4
  5.1 0.8 copy-done.4
  5.9 0.0 copy-start.5
  5.9 0.7 copy-done.5
  6.5 0.0 copy-start.6
  6.5 0.7 copy-done.6
  7.2 94.2 %shard_map.104 = (f32[32,2048]{1,0:T(8,128)S(1)}, f32[32,2048]{1,0:T(8,128)S(1)}) custom-call(s32[1]{0:T(128)S(6)} %copy.13.refs_0_, f32[4]{0:T(128)S(1)} %copy-done.6, bf16[1024,2048]{1,0:T(8,128)(2,1)} %bitcast.11, f32[32,2048]{1,0:T(8,128)S(1)} %bitcast.6, f32[32,2048]{1,0:T(8,128)S(1)} %bitcast.7, f32[32,256]{1,0:T(8,128)S(1)} %bitcast.10, ...), custom_call_target="tpu_custom_call" | custom-call | tf_op jit(solution)/shard_map/pallas_call | solution.py:558
  101.4 0.7 copy.14
  102.1 0.7 copy.15
Async XLA Ops:
  1.3 1.0 copy-start
  2.2 1.0 copy-start.1
  3.2 0.9 copy-start.2
  4.2 0.9 copy-start.3
  5.1 0.8 copy-start.4
  5.9 0.7 copy-start.5
  6.5 0.7 copy-start.6

commit v4 on v3

--- a/solution.py
+++ b/solution.py
@@ -93,19 +93,15 @@
             total = total + values[:, at : at + 128]
         return total
 
-    def accumulate(start, blocks, first):
+    def set_pivot(start, block):
+        size = block.shape[0]
+        pivot[pl.ds(start, size), :] = jnp.broadcast_to(
+            jnp.mean(block[:, :128], axis=1, keepdims=True), (size, 128)
+        )
+
+    def accumulate(start, blocks):
         size = blocks[0].shape[0]
         where = pl.ds(start, size)
-
-        def _():
-            pivot[where, :] = jnp.broadcast_to(
-                jnp.mean(blocks[0][:, :128], axis=1, keepdims=True), (size, 128)
-            )
-
-        if first is True:
-            _()
-        elif first is not None:
-            pl.when(first)(_)
         base = pivot[where, :]
         one = jnp.zeros((size, 128), F32)
         two = jnp.zeros((size, 128), F32)
@@ -129,10 +125,14 @@
             for r in range(rows):
                 start = (1 + r) * chans + k * per
                 xt[start : start + per, pl.ds(pl.multiple_of(j * step + LAG, LAG), step)] = blocks[r].astype(BF16)
-            accumulate(k * per, blocks, j == 0)
+            accumulate(k * per, blocks)
             return carry
 
-        lax.fori_loop(0, chunks, spread, 0)
+        ahead = jnp.dot(
+            perm[...], fbuf[k * 256 : (k + 1) * 256, 0:128], preferred_element_type=F32
+        )
+        set_pivot(k * per, ahead[:per])
+        lax.fori_loop(0, chunks, spread, 0, unroll=4)
 
     pl.semaphore_wait(barrier, greet)
 
@@ -223,7 +223,7 @@
             activate_block(src, row, block)
             return carry
 
-        lax.fori_loop(0, blocks_of, body, 0)
+        lax.fori_loop(0, blocks_of, body, 0, unroll=2)
 
     def activate_edge(buf, turn, row):
         side, there = (1, top) if row == 0 else (0, bottom)
@@ -288,7 +288,9 @@
                 hid[rows_at, pl.ds(start, LAG)] = rounded
                 wide_block = rounded.astype(F32)
                 kept += [wide_block[:chans], wide_block[chans:]]
-            accumulate(0, kept, pivot_now)
+            if pivot_now:
+                set_pivot(0, kept[0])
+            accumulate(0, kept)
 
         def over_cols(j, carry):
             base = j * step
@@ -298,15 +300,18 @@
             for row in beside:
                 for n in range(each):
                     activate_block(xt, row, j * each + n)
-            if isinstance(j, int):
-                keep(blocks[1:], [LAG], True if first else None)
+            if isinstance(j, int) and j == 0:
+                keep(blocks[1:], [LAG], first)
             else:
-                keep(blocks, [base, pl.multiple_of(base + LAG, LAG)], None)
+                keep(blocks, [base, base + LAG if isinstance(j, int) else pl.multiple_of(base + LAG, LAG)], False)
             return carry
 
-        over_cols(0, 0)
-        lax.fori_loop(1, chunks, over_cols, 0)
-        keep([pend[0]], [cols], None)
+        def two_chunks(n, carry):
+            return over_cols(2 * n + 1, over_cols(2 * n, carry))
+
+        over_cols(1, over_cols(0, 0))
+        lax.fori_loop(1, chunks // 2, two_chunks, 0)
+        keep([pend[0]], [cols], False)
 
     for row in (1, 2, 3):
         activate(xt, row)
@@ -562,7 +567,7 @@
         out_specs=[anywhere] * (2 if fused else 1),
         scratch_shapes=scratch,
         compiler_params=pltpu.CompilerParams(
-            collective_id=0, has_side_effects=True, vmem_limit_bytes=52 * 1024 * 1024
+            collective_id=0, has_side_effects=True, vmem_limit_bytes=62 * 1024 * 1024
         ),
     )(*[value for _, value in operands])
     advanced = result[0].reshape(outs, rows, cols)

time: 103 us -> 88.6 us (0.86)
  Pallas kernels: 94.2 us -> 83.8 us
  local copies, waits for them, and re-layouts: 7.31 us -> 3.34 us
    pallas_call x1, Pallas kernels: 94.2 us -> 83.8 us  [shards(): pl.pallas_call(functools.partial(kernel, tiles, members, fused, chans, ro...]
    unnamed x16 -> x2, local copies, waits for them, and re-layouts: 7.31 us -> 3.34 us
where the time goes in v4:
time: 88.6 us; the launch traced here: 88.4 us
  Pallas kernels  83.8 us (95%)
  local copies, waits for them, and re-layouts  3.34 us (4%)
  between operations  1.29 us (1%)
    pallas_call x1, Pallas kernels, shards(): pl.pallas_call(functools.partial(kernel, tiles, members, fused, chans, ro...  83.8 us
    unnamed x2, local copies, waits for them, and re-layouts  3.34 us

profile of v4, /device:TPU:16, one launch (start us, length us, event | category | flops | bytes accessed | tf_op | source)
XLA Modules:
  0.0 88.4 jit_solution(16543151962405744173)
XLA Ops:
  1.3 83.8 %shard_map.104 = (f32[32,2048]{1,0:T(8,128)}, f32[32,2048]{1,0:T(8,128)}) custom-call(s32[1]{0:T(128)S(6)} %copy.13.refs_0_, f32[4]{0:T(128)} %refs_1_.1, bf16[1024,2048]{1,0:T(8,128)(2,1)} %bitcast.6, f32[32,2048]{1,0:T(8,128)} %bitcast.7, f32[32,2048]{1,0:T(8,128)} %bitcast.8, f32[32,256]{1,0:T(8,128)} %bitcast.11, bf16[9,128,128]{2,1,0:T(8,128)(2,1)} %refs_6_.1, ...), custom_call_target="tpu_custom_call" | custom-call | tf_op jit(solution)/shard_map/pallas_call | solution.py:563
  85.1 1.7 %copy.14 = f32[1,4,8,2048]{3,2,1,0:T(8,128)} copy(f32[1,4,8,2048]{3,2,1,0:T(8,128)} %bitcast.10) | data formatting | bytes 524288
  86.7 1.7 %copy.15 = f32[1,4,8,2048]{3,2,1,0:T(8,128)} copy(f32[1,4,8,2048]{3,2,1,0:T(8,128)} %bitcast.9) | data formatting | bytes 524288

commit v5 on v4

--- a/solution.py
+++ b/solution.py
@@ -38,7 +38,7 @@
     (fbuf, xt, hid, wide, hw, perm, pivot, acc1, acc2, meanb, rstdb, stat, resid, noise, wa, wb,
      pend, carry_m, state, fsem, ssem, rsem, hs, hr, osem) = refs[:25]
     if fused:
-        ens_in, back_out, back_in, regr, field, es, er, bs, br = refs[25:]
+        ens_in, ens_out, back_out, back_in, gain_out, gain_in, regr, field, es, er, bs, br, gs, gr = refs[25:]
     me_t = lax.axis_index("tile")
     me_m = lax.axis_index("member")
     top = me_t > 0
@@ -223,7 +223,7 @@
             activate_block(src, row, block)
             return carry
 
-        lax.fori_loop(0, blocks_of, body, 0, unroll=2)
+        lax.fori_loop(0, blocks_of, body, 0, unroll=4)
 
     def activate_edge(buf, turn, row):
         side, there = (1, top) if row == 0 else (0, bottom)
@@ -393,7 +393,7 @@
 
     def state_copy(owner, sender):
         return pltpu.make_async_remote_copy(
-            src_ref=state.at[:, owned(owner)],
+            src_ref=ens_out.at[owner],
             dst_ref=ens_in.at[sender],
             send_sem=es.at[owner],
             recv_sem=er.at[sender],
@@ -411,36 +411,53 @@
             device_id_type=MESH,
         )
 
+    def gain_copy(owner, member):
+        return pltpu.make_async_remote_copy(
+            src_ref=gain_out,
+            dst_ref=gain_in.at[owner],
+            send_sem=gs.at[member],
+            recv_sem=gr.at[owner],
+            device_id={"member": member},
+            device_id_type=MESH,
+        )
+
     def ensemble():
         for d in range(1, members):
             other = lax.rem(me_m + d, members)
             state_copy(me_m, other).wait_recv()
+        values = [ens_in[m].astype(F32) for m in range(members)]
+        gains = []
         for o in range(outs):
             sub = pl.ds(o * rows, rows)
             one = jnp.zeros((rows, width), F32)
             two = jnp.zeros((rows, width), F32)
             for m in range(members):
-                value = ens_in[m, sub, :]
+                value = values[m][o * rows : (o + 1) * rows]
                 one = one + value
                 two = two + value * value
             mean = one / members
             var = two / members - mean * mean
             factor = jnp.sqrt(1.0 + target[o] / (var + 1.0))
-            back_out[0, sub, :] = regr[sub, :] + (mean - mean * factor)
-            back_out[1, sub, :] = factor
+            back_out[sub, :] = regr[sub, :] + (mean - mean * factor)
+            gains.append(factor - 1.0)
+        gain = jnp.concatenate(gains, axis=0)
+        gain_out[...] = gain.astype(BF16)
         for d in range(1, members):
             back_copy(me_m, lax.rem(me_m + d, members)).start()
+            gain_copy(me_m, lax.rem(me_m + d, members)).start()
         mine = pl.ds(pl.multiple_of(me_m * width, width), width)
-        field[:, mine] = back_out[0] + state[:, owned(me_m)] * back_out[1]
+        own = state[:, owned(me_m)]
+        field[:, mine] = back_out[...] + (own + own * gain)
 
     def hand_over(owner):
         @pl.when(owner != me_m)
         def _():
+            ens_out[owner] = state[:, owned(owner)].astype(BF16)
             state_copy(owner, me_m).start()
 
         @pl.when(owner == me_m)
         def _():
-            ens_in[me_m] = state[:, owned(owner)]
+            ens_in[me_m] = state[:, owned(owner)].astype(BF16)
 
     def turn_of(j, carry):
         window(j)
@@ -465,20 +482,25 @@
 
     state_out().start()
 
-    def collect(d, carry):
-        owner = lax.rem(me_m + d, members)
-        back_copy(owner, owner).wait_recv()
-        at = pl.ds(pl.multiple_of(owner * width, width), width)
-        field[:, at] = back_in[owner, 0] + state[:, owned(owner)] * back_in[owner, 1]
+    def collect(owner, carry):
+        @pl.when(owner != me_m)
+        def _():
+            back_copy(owner, owner).wait_recv()
+            gain_copy(owner, owner).wait_recv()
+            at = pl.ds(pl.multiple_of(owner * width, width), width)
+            own = state[:, owned(owner)]
+            field[:, at] = back_in[owner] + (own + own * gain_in[owner].astype(F32))
+
         return carry
 
-    lax.fori_loop(1, members, collect, 0)
+    lax.fori_loop(0, members, collect, 0)
     field_out = pltpu.make_async_copy(field, out_field, osem.at[1])
     field_out.start()
     for d in range(1, members):
         other = lax.rem(me_m + d, members)
         state_copy(other, me_m).wait_send()
         back_copy(me_m, other).wait_send()
+        gain_copy(me_m, other).wait_send()
     finish_halo(xt, 0)
     finish_halo(hid, 1)
     state_out().wait()
@@ -550,11 +572,16 @@
     ]
     if fused:
         scratch += [
+            pltpu.VMEM((members, flat, cols // members), BF16),
+            pltpu.VMEM((members, flat, cols // members), BF16),
+            pltpu.VMEM((flat, cols // members), F32),
             pltpu.VMEM((members, flat, cols // members), F32),
-            pltpu.VMEM((2, flat, cols // members), F32),
-            pltpu.VMEM((members, 2, flat, cols // members), F32),
+            pltpu.VMEM((flat, cols // members), BF16),
+            pltpu.VMEM((members, flat, cols // members), BF16),
             pltpu.VMEM((flat, cols // members), F32),
             pltpu.VMEM((flat, cols), F32),
+            dma((members,)),
+            dma((members,)),
             dma((members,)),
             dma((members,)),
             dma((members,)),

time: 88.6 us -> 77.4 us (0.87)
  the two profiles are of different devices: /device:TPU:16 before, /device:TPU:0 now
where the time goes in v5:
time: 77.4 us; the launch traced here: 77.2 us
  Pallas kernels  72.6 us (94%)
  local copies, waits for them, and re-layouts  3.34 us (4%)
  between operations  1.29 us (2%)
    pallas_call x1, Pallas kernels, shards(): pl.pallas_call(functools.partial(kernel, tiles, members, fused, chans, ro...  72.6 us
    unnamed x2, local copies, waits for them, and re-layouts  3.34 us

profile of v5, /device:TPU:0, one launch (start us, length us, event | category | flops | bytes accessed | tf_op | source)
XLA Modules:
  0.0 77.2 jit_solution(7310738820071288985)
XLA Ops:
  1.3 72.6 %shard_map.104 = (f32[32,2048]{1,0:T(8,128)}, f32[32,2048]{1,0:T(8,128)}) custom-call(s32[1]{0:T(128)S(6)} %copy.13.refs_0_, f32[4]{0:T(128)} %refs_1_.1, bf16[1024,2048]{1,0:T(8,128)(2,1)} %bitcast.6, f32[32,2048]{1,0:T(8,128)} %bitcast.7, f32[32,2048]{1,0:T(8,128)} %bitcast.8, f32[32,256]{1,0:T(8,128)} %bitcast.11, bf16[9,128,128]{2,1,0:T(8,128)(2,1)} %refs_6_.1, ...), custom_call_target="tpu_custom_call" | custom-call | tf_op jit(solution)/shard_map/pallas_call | solution.py:590
  73.9 1.7 %copy.14 = f32[1,4,8,2048]{3,2,1,0:T(8,128)} copy(f32[1,4,8,2048]{3,2,1,0:T(8,128)} %bitcast.10) | data formatting | bytes 524288
  75.5 1.7 %copy.15 = f32[1,4,8,2048]{3,2,1,0:T(8,128)} copy(f32[1,4,8,2048]{3,2,1,0:T(8,128)} %bitcast.9) | data formatting | bytes 524288

commit v6 on v5

--- a/solution.py
+++ b/solution.py
@@ -313,16 +313,16 @@
         lax.fori_loop(1, chunks // 2, two_chunks, 0)
         keep([pend[0]], [cols], False)
 
-    for row in (1, 2, 3):
+    for row in range(2, rows - 2):
         activate(xt, row)
+    first_conv(1, True, [1, rows])
     activate_edge(xt, 0, 0)
-    first_conv(0, True, [rows - 2, rows - 1, rows])
+    first_conv(0, False, [rows - 2, rows - 1])
     send_halo(hid, 1, 0)
     activate_edge(xt, 0, rows + 1)
-    middle = list(range(4, rows - 2))
-    first_conv(pairs - 1, False, middle)
+    first_conv(pairs - 1, False, [])
     send_halo(hid, 1, 1)
-    for p in range(1, pairs - 1):
+    for p in range(2, pairs - 1):
         first_conv(p, False, [])
     norm_values(1, lambda: None)
     for row in range(1, rows + 1):

time: 77.4 us -> 79.6 us (1.028)
  the two profiles are of different devices: /device:TPU:0 before, /device:TPU:16 now
where the time goes in v6:
time: 79.6 us; the launch traced here: 79 us
  Pallas kernels  74.4 us (93%)
  local copies, waits for them, and re-layouts  3.34 us (4%)
  between operations  1.29 us (2%)
    pallas_call x1, Pallas kernels, shards(): pl.pallas_call(functools.partial(kernel, tiles, members, fused, chans, ro...  74.4 us
    unnamed x2, local copies, waits for them, and re-layouts  3.34 us

profile of v6, /device:TPU:16, one launch (start us, length us, event | category | flops | bytes accessed | tf_op | source)
XLA Modules:
  0.0 79.0 jit_solution(1870156133665999227)
XLA Ops:
  1.3 74.4 %shard_map.104 = (f32[32,2048]{1,0:T(8,128)}, f32[32,2048]{1,0:T(8,128)}) custom-call(s32[1]{0:T(128)S(6)} %copy.13.refs_0_, f32[4]{0:T(128)} %refs_1_.1, bf16[1024,2048]{1,0:T(8,128)(2,1)} %bitcast.6, f32[32,2048]{1,0:T(8,128)} %bitcast.7, f32[32,2048]{1,0:T(8,128)} %bitcast.8, f32[32,256]{1,0:T(8,128)} %bitcast.11, bf16[9,128,128]{2,1,0:T(8,128)(2,1)} %refs_6_.1, ...), custom_call_target="tpu_custom_call" | custom-call | tf_op jit(solution)/shard_map/pallas_call | solution.py:590
  75.7 1.7 %copy.14 = f32[1,4,8,2048]{3,2,1,0:T(8,128)} copy(f32[1,4,8,2048]{3,2,1,0:T(8,128)} %bitcast.10) | data formatting | bytes 524288
  77.4 1.7 %copy.15 = f32[1,4,8,2048]{3,2,1,0:T(8,128)} copy(f32[1,4,8,2048]{3,2,1,0:T(8,128)} %bitcast.9) | data formatting | bytes 524288

commit v7 on v5

--- a/solution.py
+++ b/solution.py
@@ -132,7 +132,7 @@
             perm[...], fbuf[k * 256 : (k + 1) * 256, 0:128], preferred_element_type=F32
         )
         set_pivot(k * per, ahead[:per])
-        lax.fori_loop(0, chunks, spread, 0, unroll=4)
+        lax.fori_loop(0, chunks, spread, 0, unroll=8)
 
     pl.semaphore_wait(barrier, greet)
 
@@ -223,7 +223,7 @@
             activate_block(src, row, block)
             return carry
 
-        lax.fori_loop(0, blocks_of, body, 0, unroll=4)
+        lax.fori_loop(0, blocks_of, body, 0, unroll=8)
 
     def activate_edge(buf, turn, row):
         side, there = (1, top) if row == 0 else (0, bottom)

time: 77.4 us -> 74.8 us (0.966)
  the two profiles are of different devices: /device:TPU:0 before, /device:TPU:16 now
where the time goes in v7:
time: 74.8 us; the launch traced here: 73.4 us
  Pallas kernels  68.8 us (92%)
  local copies, waits for them, and re-layouts  3.34 us (4%)
  between operations  1.29 us (2%)
    pallas_call x1, Pallas kernels, shards(): pl.pallas_call(functools.partial(kernel, tiles, members, fused, chans, ro...  68.8 us
    unnamed x2, local copies, waits for them, and re-layouts  3.34 us

profile of v7, /device:TPU:16, one launch (start us, length us, event | category | flops | bytes accessed | tf_op | source)
XLA Modules:
  0.0 73.4 jit_solution(7318074859374156517)
XLA Ops:
  1.3 68.8 %shard_map.104 = (f32[32,2048]{1,0:T(8,128)}, f32[32,2048]{1,0:T(8,128)}) custom-call(s32[1]{0:T(128)S(6)} %copy.13.refs_0_, f32[4]{0:T(128)} %refs_1_.1, bf16[1024,2048]{1,0:T(8,128)(2,1)} %bitcast.6, f32[32,2048]{1,0:T(8,128)} %bitcast.7, f32[32,2048]{1,0:T(8,128)} %bitcast.8, f32[32,256]{1,0:T(8,128)} %bitcast.11, bf16[9,128,128]{2,1,0:T(8,128)(2,1)} %refs_6_.1, ...), custom_call_target="tpu_custom_call" | custom-call | tf_op jit(solution)/shard_map/pallas_call | solution.py:590
  70.1 1.7 %copy.14 = f32[1,4,8,2048]{3,2,1,0:T(8,128)} copy(f32[1,4,8,2048]{3,2,1,0:T(8,128)} %bitcast.10) | data formatting | bytes 524288
  71.7 1.7 %copy.15 = f32[1,4,8,2048]{3,2,1,0:T(8,128)} copy(f32[1,4,8,2048]{3,2,1,0:T(8,128)} %bitcast.9) | data formatting | bytes 524288
